TPU v7x, 128 devices: a whole 4x4x4 slice. The times are simulated.
128 devices in a mesh: curve: 128 (over y, x, z, core).
Axes of the slice: x: 4, y: 4, z: 4, core: 2. Of those that a mesh axis runs over, the one named last changes fastest.
Arguments:
- multipole: bfloat16 [152, 131072], P(None, 'curve'), may hold values from -6 to 6
- upward_maps: bfloat16 [8, 152, 152], replicated, may hold values from -0.15625 to 0.15625
- transfer_maps: bfloat16 [316, 152, 152], replicated, may hold values from -0.03125 to 0.03125
- downward_maps: bfloat16 [8, 152, 152], replicated, may hold values from -0.5 to 0.5
- check_inverse: bfloat16 [152, 152], replicated, may hold values from -0.5 to 0.5
- fine_lists: int32 [316, 131072], P(None, 'curve'), may hold values from -1 to 1023, as said below
- coarse_lists: int32 [316, 16384], P(None, 'curve'), may hold values from -1 to 127, as said below
Outputs:
- local_density: bfloat16 [152, 131072], P(None, 'curve')
Inputs may be any that keep to these rules, and one draw needn't show every extreme that they name: `fine_lists`: entry k of box t is -1 or the place, within its own brick, of the fine box at offset k from t; it is a place only where that box lies in the grid, its parent touches the parent of t, and both boxes are present in the tree. `coarse_lists`: entry k of box t is -1 or the place, within its own brick, of the coarse box at offset k from t; it is a place only where that box lies in the grid, its parent touches the parent of t, and both boxes are present in the tree (a coarse box is present when one of its children is).
All inputs are finite; a program needn't handle non-finite values.
Results may differ from a plain program's by a relative error of at most 0.0055.
Values may be sent and summed in bfloat16 or wider, within the bound.
A program may use at most 704 MiB of HBM per device.

v0:
```python
import jax
import jax.numpy as jnp
from jax import lax
from jax.sharding import PartitionSpec as P

BX = 8
BY = 8
BZ = 16


SHIFTS = [
    (first_axis, second_axis, third_axis)
    for first_axis in range(-3, 4)
    for second_axis in range(-3, 4)
    for third_axis in range(-3, 4)
    if max(abs(first_axis), abs(second_axis), abs(third_axis)) >= 2
]


def passed_along(shard, axis, by):
    devices = lax.axis_size(axis)
    return lax.ppermute(shard, axis, [(i, (i + by) % devices) for i in range(devices)])


def grid_counts(levels):
    return (2 ** (levels // 3), 2 ** ((levels + 1) // 3), 2 ** ((levels + 2) // 3))


def decode(position, levels):
    coords = [jnp.int32(0), jnp.int32(0), jnp.int32(0)]
    for bit_place in range(levels):
        weight = position // 2**bit_place % 2
        coords[2 - bit_place % 3] = coords[2 - bit_place % 3] + weight * 2 ** (bit_place // 3)
    return coords


def encode(coords, levels):
    encoded = jnp.int32(0)
    for bit_place in range(levels):
        encoded = encoded + coords[2 - bit_place % 3] // 2 ** (bit_place // 3) % 2 * 2**bit_place
    return encoded


def curve_steps(levels, axis_number):
    places = [bit_place for bit_place in range(levels) if 2 - bit_place % 3 == axis_number]

    def spread_bits(value):
        return sum(((value >> rank & 1) << place for rank, place in enumerate(places)))

    return [spread_bits(2**carry) - spread_bits(2**carry - 1) for carry in range(len(places))]


def extend_axis(density, axis_number, levels, anchor, position, mover, depth):
    devices = 2**levels
    limits = grid_counts(levels)
    extent = density.shape[1 + axis_number]
    lower_layers = lax.slice_in_dim(density, 0, depth, axis=1 + axis_number)
    upper_layers = lax.slice_in_dim(density, extent - depth, extent, axis=1 + axis_number)
    steps = curve_steps(levels, axis_number)
    received = []
    for facing in (-1, 1):
        sent = upper_layers if facing < 0 else lower_layers
        moved = [anchor[number] + (facing if number == axis_number else 0) for number in range(3)]
        inside = (moved[axis_number] >= 0) & (moved[axis_number] < limits[axis_number])
        wanted = jnp.mod(position - encode(moved, levels), devices)
        collected = jnp.zeros_like(sent)
        for step_size in steps:
            distance = step_size % devices if facing < 0 else -step_size % devices
            arrived = mover(sent, distance)
            collected = jnp.where(inside & (wanted == distance), arrived, collected)
        received.append(collected)
    return jnp.concatenate([received[0], density, received[1]], axis=1 + axis_number)


def fine_mover(slab, distance):
    return passed_along(slab, "curve", distance)


def coarse_mover(slab, distance):
    return passed_along(slab, "curve", distance)


def extend_all(density, levels, anchor, position, mover, depth):
    extended = density
    for axis_number in range(3):
        extended = extend_axis(extended, axis_number, levels, anchor, position, mover, depth)
    return extended


def upward(grid, upward_maps):
    channels, size_x, size_y, size_z = grid.shape
    children = (
        grid.reshape(channels, size_x // 2, 2, size_y // 2, 2, size_z // 2, 2)
        .transpose(2, 4, 6, 0, 1, 3, 5)
        .reshape(8, channels, -1)
    )
    parents = jnp.einsum(
        "opq,oqc->pc", upward_maps, children, preferred_element_type=jnp.float32
    ).astype(jnp.bfloat16)
    return parents.reshape(channels, size_x // 2, size_y // 2, size_z // 2)


def translate(extended, lists, operators, extent):
    channels = extended.shape[0]
    running = jnp.zeros((channels, extent[0] * extent[1] * extent[2]), jnp.float32)
    stride = (len(SHIFTS) + 3) // 4
    for start_at in range(0, len(SHIFTS), stride):
        chosen = SHIFTS[start_at : start_at + stride]
        stacked = jnp.stack(
            [
                extended[
                    :,
                    3 + offset[0] : 3 + offset[0] + extent[0],
                    3 + offset[1] : 3 + offset[1] + extent[1],
                    3 + offset[2] : 3 + offset[2] + extent[2],
                ].reshape(channels, -1)
                for offset in chosen
            ]
        )
        present = (lists[start_at : start_at + len(chosen)] >= 0).astype(stacked.dtype)
        stacked = stacked * present[:, None, :]
        running = running + jnp.einsum(
            "kpq,kqb->pb",
            operators[start_at : start_at + len(chosen)],
            stacked,
            preferred_element_type=jnp.float32,
        )
    return running


def local(
    multipole, upward_maps, transfer_maps, downward_maps, check_inverse, fine_lists, coarse_lists
):
    channels = multipole.shape[0]
    devices = lax.axis_size("curve")
    levels = devices.bit_length() - 1
    position = lax.axis_index("curve")
    anchor = decode(position, levels)
    fine_shape = (BX, BY, BZ)
    coarse_shape = (BX // 2, BY // 2, BZ // 2)
    fine_grid = multipole.reshape(channels, BX, BY, BZ)
    fine_extended = extend_all(fine_grid, levels, anchor, position, fine_mover, 3)
    parent_grid = upward(fine_grid, upward_maps)
    coarse_extended = extend_all(parent_grid, levels, anchor, position, coarse_mover, 3)
    coarse_check = 0.5 * translate(coarse_extended, coarse_lists, transfer_maps, coarse_shape)
    coarse_local = coarse_check.astype(jnp.bfloat16)
    fine_check = translate(fine_extended, fine_lists, transfer_maps, fine_shape)
    spread = jnp.einsum(
        "opq,qc->opc", downward_maps, coarse_local, preferred_element_type=jnp.float32
    )
    spread = (
        spread.reshape(2, 2, 2, channels, BX // 2, BY // 2, BZ // 2)
        .transpose(3, 4, 0, 5, 1, 6, 2)
        .reshape(channels, -1)
    )
    fine_total = (fine_check + spread).astype(jnp.bfloat16)
    return jnp.dot(check_inverse, fine_total, preferred_element_type=jnp.float32).astype(
        jnp.bfloat16
    )


def solution(mesh):
    placed = (P(None, "curve"), P(), P(), P(), P(), P(None, "curve"), P(None, "curve"))
    return jax.shard_map(
        local, mesh=mesh, in_specs=placed, out_specs=P(None, "curve"), check_vma=False
    )
```

profile of v0, /device:TPU:1, one launch (start us, length us, event | category | flops | bytes accessed | tf_op | source)
XLA Modules:
  0.0 722.4 jit_solution(7723143450212503590)
XLA Ops:
  3.8 6.9 collective-permute-start.16
  19.7 22.5 %fusion.102 = (bf16[79,152,152]{0,2,1:T(8,128)(2,1)}, bf16[79,152,152]{0,2,1:T(8,128)(2,1)}, bf16[79,152,152]{0,2,1:T(8,128)(2,1)}, bf16[79,152,152]{0,2,1:T(8,128)(2,1)}) fusion(bf16[316,152,152]{0,2,1:T(8,128)(2,1)} %param.9), kind=kLoop, calls=%fused_computation.745 | loop fusion | bytes 29203456 | tf_op jit(solution)/shard_map/slice | solution.py:124
  43.8 14.8 %copy.16 = bf16[79,152,152]{1,2,0:T(8,128)(2,1)} copy(bf16[79,152,152]{0,2,1:T(8,128)(2,1)} %get-tuple-element.7) | data formatting | bytes 7300864 | tf_op jit(solution)/shard_map/slice | solution.py:124
  58.6 14.8 %copy.17 = bf16[79,152,152]{1,2,0:T(8,128)(2,1)} copy(bf16[79,152,152]{0,2,1:T(8,128)(2,1)} %get-tuple-element.6) | data formatting | bytes 7300864 | tf_op jit(solution)/shard_map/slice | solution.py:124
  73.4 14.8 %copy.18 = bf16[79,152,152]{1,2,0:T(8,128)(2,1)} copy(bf16[79,152,152]{0,2,1:T(8,128)(2,1)} %get-tuple-element.8) | data formatting | bytes 7300864 | tf_op jit(solution)/shard_map/slice | solution.py:124
  88.2 14.8 %copy.19 = bf16[79,152,152]{1,2,0:T(8,128)(2,1)} copy(bf16[79,152,152]{0,2,1:T(8,128)(2,1)} %get-tuple-element.5) | data formatting | bytes 7300864 | tf_op jit(solution)/shard_map/slice | solution.py:124
  119.6 5.7 collective-permute-done.18
  125.3 4.2 collective-permute-done.19
  133.5 6.3 collective-permute-start.22
  146.9 7.0 collective-permute-start.7
  157.6 9.7 %collective-permute-start.5 = (bf16[152,14,3,16]{0,3,2,1:T(8,128)(2,1)}, bf16[152,14,3,16]{0,3,2,1:T(8,128)(2,1)}, u32[]{:S(2)}, u32[]{:S(2)}) collective-permute-start(bf16[152,14,3,16]{0,3,2,1:T(8,128)(2,1)} %get-tuple-element.331), channel_id=1, source_target_pairs={{0,2},{1,3},{2,4},{3,5},{4,6},{5,7},{6,8},{7,9},{8,10},{9,11},{10,... | collective-permute-start | bytes 612872 | tf_op jit(solution)/shard_map/ppermute | solution.py:22
  182.9 7.4 %fusion.55 = f32[128,152]{0,1:T(8,128)S(1)} fusion(bf16[79,152,152]{1,2,0:T(8,128)(2,1)S(1)} %bitcast.734, bf16[79,152,128]{1,2,0:T(8,128)(2,1)} %copy-done.284, bf16[79,128]{1,0:T(8,128)(2,1)S(1)} %copy-done.279), kind=kOutput, calls=%fused_computation.673 | convolution fusion | flops 468792320 | bytes 6822528 | tf_op jit(solution)/shard_map/kpq,kqb->pb/dot_general | solution.py:122
  190.4 4.5 fusion.76
  195.0 4.1 fusion.73
  199.1 8.7 %convolution_bitcast_fusion = f32[8,152,128]{2,1,0:T(8,128)S(1)} fusion(bf16[8,152,152]{2,1,0:T(8,128)(2,1)S(1)} %copy-done, f32[128,152]{0,1:T(8,128)S(1)} %fusion.73, bf16[79,152,152]{1,2,0:T(8,128)(2,1)} %copy.19, bf16[79,152,128]{1,2,0:T(8,128)(2,1)} %copy-done.2, bf16[79,128]{1,0:T(8,128)(2,1)S(1)} %copy-done.275), kind=kOutput, calls=%fused_computation.670 | convolution fusion | flops 516167680 | bytes 7814784 | tf_op jit(solution)/shard_map/opq,qc->opc/dot_general | solution.py:148
  234.7 4.5 collective-permute-done.8
  240.5 4.5 pad_maximum_fusion
  245.0 5.4 fusion.115
  250.5 5.7 fusion.114
  256.2 4.2 fusion.113
  260.4 4.2 fusion.112
  264.5 5.7 fusion.111
  277.7 4.9 fusion.116
  282.6 4.6 fusion.110
  287.2 5.8 fusion.109
  293.0 4.4 fusion.108
  297.4 5.4 fusion.107
  306.4 4.6 fusion.105
  386.3 38.0 %fusion.30 = f32[1024,152]{1,0:T(8,128)} fusion(bf16[79,152,152]{1,2,0:T(8,128)(2,1)S(1)} %bitcast.744, bf16[79,152,1024]{1,2,0:T(8,128)(2,1)} %constant_dynamic-update-slice_fusion.79, bf16[79,1024]{1,0:T(8,128)(2,1)S(1)} %copy-done.274), kind=kOutput, calls=%fused_computation.28 | convolution fusion | flops 3750338560 | bytes 29027200 | tf_op jit(solution)/shard_map/kpq,kqb->pb/dot_general | solution.py:122
  622.4 34.8 %fusion.27 = f32[1024,152]{1,0:T(8,128)S(1)} fusion(f32[1024,152]{1,0:T(8,128)S(1)} %copy-done.285, bf16[79,152,152]{1,2,0:T(8,128)(2,1)S(1)} %bitcast.736, bf16[79,152,1024]{1,2,0:T(8,128)(2,1)} %constant_dynamic-update-slice_fusion, bf16[79,1024]{1,0:T(8,128)(2,1)S(1)} %copy-done.273), kind=kOutput, calls=%fused_computation.27 | convolution fusion | flops 3750494208 | bytes 29649792 | tf_op jit(solution)/shard_map/kpq,kqb->pb/dot_general | solution.py:122
  657.3 37.0 %fusion.36 = f32[1024,152]{1,0:T(8,128)S(1)} fusion(f32[1024,152]{1,0:T(8,128)S(1)} %fusion.27, bf16[79,152,152]{1,2,0:T(8,128)(2,1)S(1)} %bitcast.740, bf16[79,152,1024]{1,2,0:T(8,128)(2,1)} %constant_dynamic-update-slice_fusion.158, bf16[79,1024]{1,0:T(8,128)(2,1)S(1)} %copy-done.272), kind=kOutput, calls=%fused_computation.30 | convolution fusion | flops 3750494208 | bytes 29649792 | tf_op jit(solution)/shard_map/kpq,kqb->pb/dot_general | solution.py:122
  694.4 26.7 %fusion.51 = bf16[152,1024]{0,1:T(8,128)(2,1)S(1)} fusion(f32[152,1024]{0,1:T(8,128)S(1)} %copy-done.269, f32[1024,152]{1,0:T(8,128)S(1)} %fusion.36, bf16[79,152,152]{1,2,0:T(8,128)(2,1)S(1)} %bitcast.732, bf16[79,152,1024]{1,2,0:T(8,128)(2,1)} %constant_dynamic-update-slice_fusion.237, bf16[79,1024]{1,0:T(8,128)(2,1)S(1)} %copy-done.271), kind=kOutput, calls=%fused_computation.35 | convolution fusion | flops 3750805504 | bytes 29961088 | tf_op jit(solution)/shard_map/kpq,kqb->pb/dot_general | solution.py:122
  (1349 shorter events, 371.6 us)
Async XLA Ops:
  0.0 199.0 %copy-start = (bf16[8,152,152]{2,1,0:T(8,128)(2,1)S(1)}, bf16[8,152,152]{2,1,0:T(8,128)(2,1)}, u32[]{:S(2)}) copy-start(bf16[8,152,152]{2,1,0:T(8,128)(2,1)} %param.10) | copy-start | bytes 1108996
  3.8 99.2 %collective-permute-start.16 = (bf16[152,3,4,8]{0,3,2,1:T(8,128)(2,1)}, bf16[152,3,4,8]{0,3,2,1:T(8,128)(2,1)S(1)}, u32[]{:S(2)}, u32[]{:S(2)}) collective-permute-start(bf16[152,3,4,8]{0,3,2,1:T(8,128)(2,1)} %get-tuple-element.672), channel_id=1, source_target_pairs={{0,100},{1,101},{2,102},{3,103},{4,104},{5,105},{6,106},{7,107},{8... | collective-permute-start | bytes 87560 | tf_op jit(solution)/shard_map/ppermute | solution.py:22
  10.6 95.8 %collective-permute-start.17 = (bf16[152,3,4,8]{0,3,2,1:T(8,128)(2,1)}, bf16[152,3,4,8]{0,3,2,1:T(8,128)(2,1)S(1)}, u32[]{:S(2)}, u32[]{:S(2)}) collective-permute-start(bf16[152,3,4,8]{0,3,2,1:T(8,128)(2,1)} %get-tuple-element.672), channel_id=1, source_target_pairs={{0,124},{1,125},{2,126},{3,127},{4,0},{5,1},{6,2},{7,3},{8,4},{9,5... | collective-permute-start | bytes 87560 | tf_op jit(solution)/shard_map/ppermute | solution.py:22
  12.8 96.5 %collective-permute-start.14 = (bf16[152,3,4,8]{0,3,2,1:T(8,128)(2,1)S(1)}, bf16[152,3,4,8]{0,3,2,1:T(8,128)(2,1)S(1)}, u32[]{:S(2)}, u32[]{:S(2)}) collective-permute-start(bf16[152,3,4,8]{0,3,2,1:T(8,128)(2,1)S(1)} %get-tuple-element.671), channel_id=1, source_target_pairs={{0,28},{1,29},{2,30},{3,31},{4,32},{5,33},{6,34},{7,35},{8,36},{9,... | collective-permute-start | bytes 87560 | tf_op jit(solution)/shard_map/ppermute | solution.py:22
  15.8 93.5 %collective-permute-start.15 = (bf16[152,3,4,8]{0,3,2,1:T(8,128)(2,1)S(1)}, bf16[152,3,4,8]{0,3,2,1:T(8,128)(2,1)S(1)}, u32[]{:S(2)}, u32[]{:S(2)}) collective-permute-start(bf16[152,3,4,8]{0,3,2,1:T(8,128)(2,1)S(1)} %get-tuple-element.671), channel_id=1, source_target_pairs={{0,4},{1,5},{2,6},{3,7},{4,8},{5,9},{6,10},{7,11},{8,12},{9,13},{1... | collective-permute-start | bytes 87560 | tf_op jit(solution)/shard_map/ppermute | solution.py:22
  15.8 115.9 %collective-permute-start.2 = (bf16[152,3,8,16]{0,3,2,1:T(8,128)(2,1)S(1)}, bf16[152,3,8,16]{0,3,2,1:T(8,128)(2,1)S(1)}, u32[]{:S(2)}, u32[]{:S(2)}) collective-permute-start(bf16[152,3,8,16]{0,3,2,1:T(8,128)(2,1)S(1)} %get-tuple-element.616), channel_id=1, source_target_pairs={{0,100},{1,101},{2,102},{3,103},{4,104},{5,105},{6,106},{7,107},{8... | collective-permute-start | bytes 350216 | tf_op jit(solution)/shard_map/ppermute | solution.py:22
  102.9 30.5 %collective-permute-start.3 = (bf16[152,3,8,16]{0,3,2,1:T(8,128)(2,1)S(1)}, bf16[152,3,8,16]{0,3,2,1:T(8,128)(2,1)S(1)}, u32[]{:S(2)}, u32[]{:S(2)}) collective-permute-start(bf16[152,3,8,16]{0,3,2,1:T(8,128)(2,1)S(1)} %get-tuple-element.616), channel_id=1, source_target_pairs={{0,124},{1,125},{2,126},{3,127},{4,0},{5,1},{6,2},{7,3},{8,4},{9,5... | collective-permute-start | bytes 350216 | tf_op jit(solution)/shard_map/ppermute | solution.py:22
  106.5 27.1 %collective-permute-start = (bf16[152,3,8,16]{0,3,2,1:T(8,128)(2,1)S(1)}, bf16[152,3,8,16]{0,3,2,1:T(8,128)(2,1)S(1)}, u32[]{:S(2)}, u32[]{:S(2)}) collective-permute-start(bf16[152,3,8,16]{0,3,2,1:T(8,128)(2,1)S(1)} %get-tuple-element.615), channel_id=1, source_target_pairs={{0,28},{1,29},{2,30},{3,31},{4,32},{5,33},{6,34},{7,35},{8,36},{9,... | collective-permute-start | bytes 350216 | tf_op jit(solution)/shard_map/ppermute | solution.py:22
  109.4 7.2 collective-permute-start.20
  111.4 7.8 %collective-permute-start.21 = (bf16[152,10,3,8]{0,3,2,1:T(8,128)(2,1)S(1)}, bf16[152,10,3,8]{0,3,2,1:T(8,128)(2,1)S(1)}, u32[]{:S(2)}, u32[]{:S(2)}) collective-permute-start(bf16[152,10,3,8]{0,3,2,1:T(8,128)(2,1)S(1)} %get-tuple-element.664), channel_id=1, source_target_pairs={{0,126},{1,127},{2,0},{3,1},{4,2},{5,3},{6,4},{7,5},{8,6},{9,7},{1... | collective-permute-start | bytes 218888 | tf_op jit(solution)/shard_map/ppermute | solution.py:22
  116.6 8.7 %collective-permute-start.18 = (bf16[152,10,3,8]{0,3,2,1:T(8,128)(2,1)S(1)}, bf16[152,10,3,8]{0,3,2,1:T(8,128)(2,1)S(1)}, u32[]{:S(2)}, u32[]{:S(2)}) collective-permute-start(bf16[152,10,3,8]{0,3,2,1:T(8,128)(2,1)S(1)} %get-tuple-element.663), channel_id=1, source_target_pairs={{0,14},{1,15},{2,16},{3,17},{4,18},{5,19},{6,20},{7,21},{8,22},{9,... | collective-permute-start | bytes 218888 | tf_op jit(solution)/shard_map/ppermute | solution.py:22
  119.2 10.3 %collective-permute-start.19 = (bf16[152,10,3,8]{0,3,2,1:T(8,128)(2,1)S(1)}, bf16[152,10,3,8]{0,3,2,1:T(8,128)(2,1)S(1)}, u32[]{:S(2)}, u32[]{:S(2)}) collective-permute-start(bf16[152,10,3,8]{0,3,2,1:T(8,128)(2,1)S(1)} %get-tuple-element.663), channel_id=1, source_target_pairs={{0,2},{1,3},{2,4},{3,5},{4,6},{5,7},{6,8},{7,9},{8,10},{9,11},{10,... | collective-permute-start | bytes 218888 | tf_op jit(solution)/shard_map/ppermute | solution.py:22
  125.3 14.5 %collective-permute-start.1 = (bf16[152,3,8,16]{0,3,2,1:T(8,128)(2,1)S(1)}, bf16[152,3,8,16]{0,3,2,1:T(8,128)(2,1)S(1)}, u32[]{:S(2)}, u32[]{:S(2)}) collective-permute-start(bf16[152,3,8,16]{0,3,2,1:T(8,128)(2,1)S(1)} %get-tuple-element.615), channel_id=1, source_target_pairs={{0,4},{1,5},{2,6},{3,7},{4,8},{5,9},{6,10},{7,11},{8,12},{9,13},{1... | collective-permute-start | bytes 350216 | tf_op jit(solution)/shard_map/ppermute | solution.py:22
  129.9 14.1 %collective-permute-start.25 = (bf16[152,10,10,3]{0,3,2,1:T(4,128)(2,1)S(1)}, bf16[152,10,10,3]{0,3,2,1:T(4,128)(2,1)S(1)}, u32[]{:S(2)}, u32[]{:S(2)}) collective-permute-start(bf16[152,10,10,3]{0,3,2,1:T(4,128)(2,1)S(1)} %get-tuple-element.619), channel_id=1, source_target_pairs={{0,73},{1,74},{2,75},{3,76},{4,77},{5,78},{6,79},{7,80},{8,81},{9,... | collective-permute-start | bytes 273608 | tf_op jit(solution)/shard_map/ppermute | solution.py:22
  131.8 15.1 %collective-permute-start.26 = (bf16[152,10,10,3]{0,3,2,1:T(4,128)(2,1)S(1)}, bf16[152,10,10,3]{0,3,2,1:T(4,128)(2,1)S(1)}, u32[]{:S(2)}, u32[]{:S(2)}) collective-permute-start(bf16[152,10,10,3]{0,3,2,1:T(4,128)(2,1)S(1)} %get-tuple-element.619), channel_id=1, source_target_pairs={{0,121},{1,122},{2,123},{3,124},{4,125},{5,126},{6,127},{7,0},{8,1... | collective-permute-start | bytes 273608 | tf_op jit(solution)/shard_map/ppermute | solution.py:22
  133.5 13.4 %collective-permute-start.27 = (bf16[152,10,10,3]{0,3,2,1:T(4,128)(2,1)S(1)}, bf16[152,10,10,3]{0,3,2,1:T(4,128)(2,1)S(1)}, u32[]{:S(2)}, u32[]{:S(2)}) collective-permute-start(bf16[152,10,10,3]{0,3,2,1:T(4,128)(2,1)S(1)} %get-tuple-element.619), channel_id=1, source_target_pairs={{0,127},{1,0},{2,1},{3,2},{4,3},{5,4},{6,5},{7,6},{8,7},{9,8},{10,... | collective-permute-start | bytes 273608 | tf_op jit(solution)/shard_map/ppermute | solution.py:22
  133.5 20.6 %collective-permute-start.22 = (bf16[152,10,10,3]{0,3,2,1:T(4,128)(2,1)S(1)}, bf16[152,10,10,3]{0,3,2,1:T(4,128)(2,1)S(1)}, u32[]{:S(2)}, u32[]{:S(2)}) collective-permute-start(bf16[152,10,10,3]{0,3,2,1:T(4,128)(2,1)S(1)} %get-tuple-element.620), channel_id=1, source_target_pairs={{0,55},{1,56},{2,57},{3,58},{4,59},{5,60},{6,61},{7,62},{8,63},{9,... | collective-permute-start | bytes 273608 | tf_op jit(solution)/shard_map/ppermute | solution.py:22
  139.8 17.8 %collective-permute-start.23 = (bf16[152,10,10,3]{0,3,2,1:T(4,128)(2,1)S(1)}, bf16[152,10,10,3]{0,3,2,1:T(4,128)(2,1)S(1)}, u32[]{:S(2)}, u32[]{:S(2)}) collective-permute-start(bf16[152,10,10,3]{0,3,2,1:T(4,128)(2,1)S(1)} %get-tuple-element.620), channel_id=1, source_target_pairs={{0,7},{1,8},{2,9},{3,10},{4,11},{5,12},{6,13},{7,14},{8,15},{9,16}... | collective-permute-start | bytes 273608 | tf_op jit(solution)/shard_map/ppermute | solution.py:22
  144.0 23.3 %collective-permute-start.24 = (bf16[152,10,10,3]{0,3,2,1:T(4,128)(2,1)S(1)}, bf16[152,10,10,3]{0,3,2,1:T(4,128)(2,1)S(1)}, u32[]{:S(2)}, u32[]{:S(2)}) collective-permute-start(bf16[152,10,10,3]{0,3,2,1:T(4,128)(2,1)S(1)} %get-tuple-element.620), channel_id=1, source_target_pairs={{0,1},{1,2},{2,3},{3,4},{4,5},{5,6},{6,7},{7,8},{8,9},{9,10},{10,1... | collective-permute-start | bytes 273608 | tf_op jit(solution)/shard_map/ppermute | solution.py:22
  146.9 66.0 %collective-permute-start.6 = (bf16[152,14,3,16]{0,3,2,1:T(8,128)(2,1)}, bf16[152,14,3,16]{0,3,2,1:T(8,128)(2,1)S(1)}, u32[]{:S(2)}, u32[]{:S(2)}) collective-permute-start(bf16[152,14,3,16]{0,3,2,1:T(8,128)(2,1)} %get-tuple-element.332), channel_id=1, source_target_pairs={{0,114},{1,115},{2,116},{3,117},{4,118},{5,119},{6,120},{7,121},{8... | collective-permute-start | bytes 612872 | tf_op jit(solution)/shard_map/ppermute | solution.py:22
  146.9 66.0 %collective-permute-start.7 = (bf16[152,14,3,16]{0,3,2,1:T(8,128)(2,1)}, bf16[152,14,3,16]{0,3,2,1:T(8,128)(2,1)}, u32[]{:S(2)}, u32[]{:S(2)}) collective-permute-start(bf16[152,14,3,16]{0,3,2,1:T(8,128)(2,1)} %get-tuple-element.332), channel_id=1, source_target_pairs={{0,126},{1,127},{2,0},{3,1},{4,2},{5,3},{6,4},{7,5},{8,6},{9,7},{1... | collective-permute-start | bytes 612872 | tf_op jit(solution)/shard_map/ppermute | solution.py:22
  154.1 59.8 %collective-permute-start.4 = (bf16[152,14,3,16]{0,3,2,1:T(8,128)(2,1)}, bf16[152,14,3,16]{0,3,2,1:T(8,128)(2,1)}, u32[]{:S(2)}, u32[]{:S(2)}) collective-permute-start(bf16[152,14,3,16]{0,3,2,1:T(8,128)(2,1)} %get-tuple-element.331), channel_id=1, source_target_pairs={{0,14},{1,15},{2,16},{3,17},{4,18},{5,19},{6,20},{7,21},{8,22},{9,... | collective-permute-start | bytes 612872 | tf_op jit(solution)/shard_map/ppermute | solution.py:22
  157.6 56.3 %collective-permute-start.5 = (bf16[152,14,3,16]{0,3,2,1:T(8,128)(2,1)}, bf16[152,14,3,16]{0,3,2,1:T(8,128)(2,1)}, u32[]{:S(2)}, u32[]{:S(2)}) collective-permute-start(bf16[152,14,3,16]{0,3,2,1:T(8,128)(2,1)} %get-tuple-element.331), channel_id=1, source_target_pairs={{0,2},{1,3},{2,4},{3,5},{4,6},{5,7},{6,8},{7,9},{8,10},{9,11},{10,... | collective-permute-start | bytes 612872 | tf_op jit(solution)/shard_map/ppermute | solution.py:22
  214.3 18.2 %collective-permute-start.11 = (bf16[152,14,14,3]{0,3,2,1:T(4,128)(2,1)S(1)}, bf16[152,14,14,3]{0,3,2,1:T(4,128)(2,1)S(1)}, u32[]{:S(2)}, u32[]{:S(2)}) collective-permute-start(bf16[152,14,14,3]{0,3,2,1:T(4,128)(2,1)S(1)} %get-tuple-element.287), channel_id=1, source_target_pairs={{0,73},{1,74},{2,75},{3,76},{4,77},{5,78},{6,79},{7,80},{8,81},{9,... | collective-permute-start | bytes 536264 | tf_op jit(solution)/shard_map/ppermute | solution.py:22
  214.4 20.0 %collective-permute-start.12 = (bf16[152,14,14,3]{0,3,2,1:T(4,128)(2,1)S(1)}, bf16[152,14,14,3]{0,3,2,1:T(4,128)(2,1)S(1)}, u32[]{:S(2)}, u32[]{:S(2)}) collective-permute-start(bf16[152,14,14,3]{0,3,2,1:T(4,128)(2,1)S(1)} %get-tuple-element.287), channel_id=1, source_target_pairs={{0,121},{1,122},{2,123},{3,124},{4,125},{5,126},{6,127},{7,0},{8,1... | collective-permute-start | bytes 536264 | tf_op jit(solution)/shard_map/ppermute | solution.py:22
  214.5 19.9 %collective-permute-start.13 = (bf16[152,14,14,3]{0,3,2,1:T(4,128)(2,1)S(1)}, bf16[152,14,14,3]{0,3,2,1:T(4,128)(2,1)S(1)}, u32[]{:S(2)}, u32[]{:S(2)}) collective-permute-start(bf16[152,14,14,3]{0,3,2,1:T(4,128)(2,1)S(1)} %get-tuple-element.287), channel_id=1, source_target_pairs={{0,127},{1,0},{2,1},{3,2},{4,3},{5,4},{6,5},{7,6},{8,7},{9,8},{10,... | collective-permute-start | bytes 536264 | tf_op jit(solution)/shard_map/ppermute | solution.py:22
  214.6 24.7 %collective-permute-start.8 = (bf16[152,14,14,3]{0,3,2,1:T(4,128)(2,1)S(1)}, bf16[152,14,14,3]{0,3,2,1:T(4,128)(2,1)S(1)}, u32[]{:S(2)}, u32[]{:S(2)}) collective-permute-start(bf16[152,14,14,3]{0,3,2,1:T(4,128)(2,1)S(1)} %get-tuple-element.288), channel_id=1, source_target_pairs={{0,55},{1,56},{2,57},{3,58},{4,59},{5,60},{6,61},{7,62},{8,63},{9,... | collective-permute-start | bytes 536264 | tf_op jit(solution)/shard_map/ppermute | solution.py:22
  218.2 22.0 %collective-permute-start.9 = (bf16[152,14,14,3]{0,3,2,1:T(4,128)(2,1)S(1)}, bf16[152,14,14,3]{0,3,2,1:T(4,128)(2,1)S(1)}, u32[]{:S(2)}, u32[]{:S(2)}) collective-permute-start(bf16[152,14,14,3]{0,3,2,1:T(4,128)(2,1)S(1)} %get-tuple-element.288), channel_id=1, source_target_pairs={{0,7},{1,8},{2,9},{3,10},{4,11},{5,12},{6,13},{7,14},{8,15},{9,16}... | collective-permute-start | bytes 536264 | tf_op jit(solution)/shard_map/ppermute | solution.py:22
  232.5 7.7 %collective-permute-start.10 = (bf16[152,14,14,3]{0,3,2,1:T(4,128)(2,1)S(1)}, bf16[152,14,14,3]{0,3,2,1:T(4,128)(2,1)S(1)}, u32[]{:S(2)}, u32[]{:S(2)}) collective-permute-start(bf16[152,14,14,3]{0,3,2,1:T(4,128)(2,1)S(1)} %get-tuple-element.288), channel_id=1, source_target_pairs={{0,1},{1,2},{2,3},{3,4},{4,5},{5,6},{6,7},{7,8},{8,9},{9,10},{10,1... | collective-permute-start | bytes 536264 | tf_op jit(solution)/shard_map/ppermute | solution.py:22
  386.3 40.6 %copy-start.195 = (bf16[152,8,8,16]{0,3,2,1:T(8,128)(2,1)S(1)}, bf16[152,8,8,16]{0,3,2,1:T(8,128)(2,1)}, u32[]{:S(2)}) copy-start(bf16[152,8,8,16]{0,3,2,1:T(8,128)(2,1)} %get-tuple-element.270) | copy-start | bytes 933892
  386.3 41.5 %copy-start.193 = (bf16[152,8,8,16]{0,3,2,1:T(8,128)(2,1)S(1)}, bf16[152,8,8,16]{0,3,2,1:T(8,128)(2,1)}, u32[]{:S(2)}) copy-start(bf16[152,8,8,16]{0,3,2,1:T(8,128)(2,1)} %get-tuple-element.269) | copy-start | bytes 933892
  622.4 71.9 %slice-start = ((s8[6148096]{0:T(1024)(128)(4,1)}), s8[4194304]{0:T(1024)(128)(4,1)S(1)}, s32[]{:S(2)}) async-start(s8[6148096]{0:T(1024)(128)(4,1)} %bitcast.731), calls=%async_computation | async-start | bytes 8388608
  (296 other events, 2795.1 us)
where the time goes:
time: 736 us; the launch traced here: 722 us
  local copies, waits for them, and re-layouts  448 us (61%)
  matrix products  164 us (22%)
  starting transfers between devices  68.6 us (9%)
  waiting for transfers between devices  25.8 us (4%)
  other arithmetic  12.5 us (2%)
    unnamed x1225, local copies, waits for them, and re-layouts  277 us
    dot_general x7, matrix products, translate(): jnp.einsum('kpq,kqb->pb', operators[start_at:start_at + len(chosen)], sta...  152 us
    slice x5, local copies, waits for them, and re-layouts, translate(): operators[start_at:start_at + len(chosen)]  81.6 us
    slice x36, local copies, waits for them, and re-layouts, translate(): extended[:, 3 + offset[0]:3 + offset[0] + extent[0], 3 + offset[1]:3 + of...  79.2 us
    ppermute x28, starting transfers between devices, passed_along(): lax.ppermute(shard, axis, [(i, (i + by) % devices) for i in range(devices)])  68.6 us
    ppermute x28, waiting for transfers between devices, passed_along(): lax.ppermute(shard, axis, [(i, (i + by) % devices) for i in range(devices)])  25.8 us
  transfers between devices with their start and end apart: 28, of which 8 were waited for; matrix products, arithmetic and copies ran while one was open for 18% of the time, Pallas kernels for 0%

commit v1 on v0

v1 whole, which is shorter than its diff:
```python
import functools

import jax
import jax.numpy as jnp
import numpy as np
from jax import lax
from jax.experimental import pallas as pl
from jax.experimental.pallas import tpu as pltpu
from jax.sharding import PartitionSpec as P

Q = 152
OFFS = 316
F32 = jnp.float32
BF16 = jnp.bfloat16
NN = (((1,), (0,)), ((), ()))
NT = (((1,), (1,)), ((), ()))
TN = (((0,), (0,)), ((), ()))
MESH = pl.DeviceIdType.MESH

SHIFTS = [
    (i, j, k)
    for i in range(-3, 4)
    for j in range(-3, 4)
    for k in range(-3, 4)
    if max(abs(i), abs(j), abs(k)) >= 2
]
NUMBER = {offset: number for number, offset in enumerate(SHIFTS)}
SIDES = [(i, j, k) for i in (-1, 0, 1) for j in (-1, 0, 1) for k in (-1, 0, 1)]
OCTANTS = [(a, b, c) for a in (0, 1) for b in (0, 1) for c in (0, 1)]


def piece_rows(side):
    ranges = []
    for component, extent in zip(side, (4, 4, 8)):
        ranges.append({-1: [extent - 1], 0: list(range(extent)), 1: [0]}[component])
    return [(x, y, z) for x in ranges[0] for y in ranges[1] for z in ranges[2]]


def piece_places():
    places, row = {}, 0
    order = [s for s in SIDES if s[0] == -1] + [(0, 0, 0)] + [s for s in SIDES if s[0] == 0 and s != (0, 0, 0)]
    order += [s for s in SIDES if s[0] == 1]
    for side in order:
        size = -(-len(piece_rows(side)) // 16) * 16
        places[side] = (row, size)
        row += size
    return places, row


PLACES, ROWS = piece_places()
OWN = PLACES[(0, 0, 0)][0]
SPAN = {-1: (0, OWN + 288), 0: (OWN, OWN + 288), 1: (OWN, ROWS)}


def send_picks():
    picks = np.zeros((ROWS, 128), np.float32)
    for side, (row, _) in PLACES.items():
        for number, (x, y, z) in enumerate(piece_rows(side)):
            picks[row + number, x * 32 + y * 8 + z] = 1
    return picks


def window_rows():
    rows = np.zeros((27, 128), np.int32)
    for number, shift in enumerate(SIDES):
        for x in range(4):
            for y in range(4):
                for z in range(8):
                    at = (x + shift[0], y + shift[1], z + shift[2])
                    side = tuple((-1 if c < 0 else 1 if c >= e else 0) for c, e in zip(at, (4, 4, 8)))
                    wrapped = tuple(c % e for c, e in zip(at, (4, 4, 8)))
                    rows[number, x * 32 + y * 8 + z] = PLACES[side][0] + piece_rows(side).index(wrapped)
    return rows


def coarse_window_picks():
    picks = np.zeros((27 * 16, 27 * 16), np.float32)
    for number, shift in enumerate(SIDES):
        for x in range(2):
            for y in range(2):
                for z in range(4):
                    at = (x + shift[0], y + shift[1], z + shift[2])
                    side = tuple((-1 if c < 0 else 1 if c >= e else 0) for c, e in zip(at, (2, 2, 4)))
                    wrapped = tuple(c % e for c, e in zip(at, (2, 2, 4)))
                    row = SIDES.index(side) * 16 + wrapped[0] * 8 + wrapped[1] * 4 + wrapped[2]
                    picks[number * 16 + x * 8 + y * 4 + z, row] = 1
    return picks


def fine_places():
    places = np.zeros((1, 1024), np.int32)
    for o, (a, b, c) in enumerate(OCTANTS):
        for x in range(4):
            for y in range(4):
                for z in range(8):
                    places[0, o * 128 + x * 32 + y * 8 + z] = ((2 * x + a) * 8 + 2 * y + b) * 16 + 2 * z + c
    return places


def coarse_picks():
    picks = np.zeros((128, 128), np.float32)
    for o, (a, b, c) in enumerate(OCTANTS):
        for x in range(2):
            for y in range(2):
                for z in range(4):
                    picks[o * 16 + x * 8 + y * 4 + z, ((2 * x + a) * 4 + 2 * y + b) * 8 + 2 * z + c] = 1
    return picks


def window_of(offset, octant):
    direction, source = [], []
    for d, a in zip(offset, octant):
        direction.append(min(1, max(-1, (a + d) // 2)))
        source.append((a + d) % 2)
    number = (direction[0] + 1) * 9 + (direction[1] + 1) * 3 + direction[2] + 1
    return number * 8 + source[0] * 4 + source[1] * 2 + source[2]


def kind(component):
    return 0 if abs(component) < 3 else component


def groups():
    by_kind = {}
    for offset in SHIFTS:
        by_kind.setdefault(tuple(kind(c) for c in offset), []).append(offset)

    def octants_of(kinds):
        return [o for o in OCTANTS if all(k == 0 or (k == 3) == (a == 0) for k, a in zip(kinds, o))]

    middle = by_kind[(0, 0, 0)]
    cuts = [[o for o in middle if o[0] == -2]]
    inner = [o for o in middle if abs(o[0]) < 2]
    cuts += [inner[:25], inner[25:] + [None, None], [o for o in middle if o[0] == 2]]
    eight = [(cut, OCTANTS) for cut in cuts]
    four, two = [], []
    for kinds, offsets in sorted(by_kind.items()):
        edges = sum(k != 0 for k in kinds)
        if edges == 1:
            four.append((offsets, octants_of(kinds)))
        if edges == 2:
            offsets = list(offsets)
            if kinds[2] == 0:
                offsets += by_kind[kinds[:2] + (-3,)] + by_kind[kinds[:2] + (3,)]
            two.append((offsets + [None] * (8 - len(offsets)), octants_of(kinds)))
    return eight, four, two


def table(members):
    slots, octants = [], []
    for offsets, octs in members:
        octants += [OCTANTS.index(o) for o in octs]
        for offset in offsets:
            if offset is None:
                slots += [NUMBER[offsets[0]], OFFS] + [window_of(offsets[0], o) for o in octs]
            else:
                slots += [NUMBER[offset], NUMBER[offset]] + [window_of(offset, o) for o in octs]
    return np.array(slots, np.int32), np.array(octants, np.int32)


EIGHT, FOUR, TWO = groups()
PLANES = [(min(n for n, o in enumerate(SHIFTS) if o[0] == d), sum(o[0] == d for o in SHIFTS)) for d in range(-3, 4)]
PLANE_ORDER = [1, 2, 3, 4, 5, 0, 6]


def neighbour(me, shift):
    def bit(place):
        return me // 2**place % 2

    x = (bit(2) + 2 * bit(5) + shift[0] + 4) % 4
    y = (bit(1) + 2 * bit(4) + shift[1] + 4) % 4
    z = (bit(0) + 2 * bit(3) + 4 * bit(6) + shift[2] + 8) % 8
    return (
        z % 2 + 2 * (y % 2) + 4 * (x % 2) + 8 * (z // 2 % 2) + 16 * (y // 2) + 32 * (x // 2) + 64 * (z // 4)
    )


def spread_lanes(blocks, copies=False):
    gap = jnp.zeros((blocks[0].shape[0], 8), blocks[0].dtype)
    return jnp.concatenate([part for block in blocks for part in (block, gap)], axis=1)


def exchange_kernel(mult, up, picks, cpicks, ef, ec, sent, csent, send, recv, csend, crecv):
    me = lax.axis_index("curve")
    others = [s for s in SIDES if s != (0, 0, 0)]
    barrier = pltpu.get_barrier_semaphore()
    for side in others:
        pl.semaphore_signal(barrier, inc=1, device_id=(neighbour(me, side),), device_id_type=MESH)

    row = lax.broadcasted_iota(jnp.int32, (128, 1), 0)
    base = row // 32 * 256 + row // 8 % 4 * 32 + row % 8 * 2
    lane = lax.broadcasted_iota(jnp.int32, (128, 1024), 1)
    rests, coarse = [], jnp.zeros((128, Q), F32)
    for o, (a, b, c) in enumerate(OCTANTS):
        pick = (lane == base + (a * 128 + b * 16 + c)).astype(F32).astype(BF16)
        child = lax.dot_general(pick, mult[...], NT, preferred_element_type=F32)
        ef[OWN : OWN + 128, o * 128 : (o + 1) * 128] = child[:, :128].astype(BF16)
        rests.append(child[:, 128:])
        coarse += lax.dot_general(child.astype(BF16), up[o], NT, preferred_element_type=F32)
    ef[OWN : OWN + 128, 1024:1280] = spread_lanes(rests).astype(BF16)
    sent[...] = lax.dot_general(
        picks[...], ef[OWN : OWN + 128, :], NN, preferred_element_type=F32
    ).astype(BF16)

    pl.semaphore_wait(barrier, 26)
    copies = []
    for number, side in enumerate(others):
        start, size = PLACES[side]
        to = neighbour(me, tuple(-c for c in side))
        copies.append(
            pltpu.make_async_remote_copy(
                src_ref=sent.at[pl.ds(start, size)],
                dst_ref=ef.at[pl.ds(start, size)],
                send_sem=send.at[number],
                recv_sem=recv.at[number],
                device_id=(to,),
                device_id_type=MESH,
            )
        )
        copies[-1].start()

    coarse = coarse.astype(BF16)
    rests = []
    mine = lax.dot_general(cpicks[...], coarse, NN, preferred_element_type=F32)
    for o in range(8):
        csent[:, o * 128 : (o + 1) * 128] = mine[o * 16 : (o + 1) * 16, :128].astype(BF16)
        rests.append(mine[o * 16 : (o + 1) * 16, 128:])
    csent[:, 1024:1280] = spread_lanes(rests).astype(BF16)
    for number, side in enumerate(others):
        to = neighbour(me, tuple(-c for c in side))
        copies.append(
            pltpu.make_async_remote_copy(
                src_ref=csent,
                dst_ref=ec.at[SIDES.index(side)],
                send_sem=csend.at[number],
                recv_sem=crecv.at[number],
                device_id=(to,),
                device_id_type=MESH,
            )
        )
        copies[-1].start()
    ec[13] = csent[...]
    for copy in copies:
        copy.wait()


def exchange(multipole, upward_maps):
    vmem = pl.BlockSpec(memory_space=pltpu.VMEM)
    return pl.pallas_call(
        exchange_kernel,
        out_shape=[
            jax.ShapeDtypeStruct((ROWS, 1280), BF16),
            jax.ShapeDtypeStruct((27, 16, 1280), BF16),
        ],
        in_specs=[vmem] * 4,
        out_specs=[vmem] * 2,
        scratch_shapes=[
            pltpu.VMEM((ROWS, 1280), BF16),
            pltpu.VMEM((16, 1280), BF16),
            pltpu.SemaphoreType.DMA((26,)),
            pltpu.SemaphoreType.DMA((26,)),
            pltpu.SemaphoreType.DMA((26,)),
            pltpu.SemaphoreType.DMA((26,)),
        ],
        compiler_params=pltpu.CompilerParams(
            collective_id=0, has_side_effects=True, vmem_limit_bytes=40 << 20
        ),
        name="exchange",
    )(multipole, upward_maps, jnp.asarray(send_picks(), BF16), jnp.asarray(coarse_picks(), BF16))


def translate_kernel(
    t8, o8, t4, o4, t2, o2, ef, ec, maps, fine_lists, coarse_lists, down, inverse,
    wrows, wcpicks, places, cpicks, out,
    mbuf, window, cmain, crest, mask, cmask, perm, lhs, rhs, crhs, acc, cacc, sems,
):
    loads = [
        pltpu.make_async_copy(maps.at[pl.ds(*PLANES[n])], mbuf.at[pl.ds(*PLANES[n])], sems.at[n])
        for n in range(7)
    ]
    for n in PLANE_ORDER:
        loads[n].start()

    for at in range(0, 1024, 128):
        box = lax.broadcasted_iota(jnp.int32, (128, 1024), 0) + at
        perm[at : at + 128, :] = (box == places[...]).astype(F32).astype(BF16)

    present = (fine_lists[...] >= 0).astype(F32).astype(BF16)
    for o in range(8):
        mask[o, 0:OFFS, :] = lax.dot_general(
            present, perm[:, o * 128 : (o + 1) * 128], NN, preferred_element_type=F32
        )
        mask[o, OFFS : OFFS + 4, :] = jnp.zeros((4, 128), F32)
    cmask[0:OFFS, :] = (coarse_lists[...] >= 0).astype(F32)
    cmask[OFFS : OFFS + 4, :] = jnp.zeros((4, 128), F32)

    for dx in (-1, 0, 1):
        first, last = SPAN[dx]
        iota = lax.broadcasted_iota(jnp.int32, (last - first, 1152), 0) + first
        pick = (iota == wrows[:, (dx + 1) * 1152 : (dx + 2) * 1152]).astype(F32).astype(BF16)

        def block(i, _, first=first, last=last, pick=pick, dx=dx):
            lanes = pl.ds(pl.multiple_of(i * 128, 128), 128)
            got = lax.dot_general(
                ef[first:last, lanes], pick, TN, preferred_element_type=F32
            ).astype(BF16)
            for n in range(9):
                window[((dx + 1) * 9 + n) * 8 + i, 0:128, :] = got[:, n * 128 : (n + 1) * 128]
            return 0

        lax.fori_loop(0, 8, block, 0)
        for half in range(2):
            got = lax.dot_general(
                ef[first:last, 1024 + half * 128 : 1152 + half * 128], pick, TN, preferred_element_type=F32
            ).astype(BF16)
            for n in range(9):
                for c in range(4):
                    window[((dx + 1) * 9 + n) * 8 + half * 4 + c, 128:160, :] = got[
                        c * 32 : (c + 1) * 32, n * 128 : (n + 1) * 128
                    ]

    source = ec[...].reshape(27 * 16, 1280)
    for c in range(8):
        got = lax.dot_general(
            wcpicks[...], source[:, c * 128 : (c + 1) * 128], NN, preferred_element_type=F32
        ).astype(BF16)
        rest = lax.dot_general(
            wcpicks[...], source[:, 1024 + c * 32 : 1056 + c * 32], NN, preferred_element_type=F32
        )
        rest = jnp.concatenate([rest] * 4, axis=1).astype(BF16)
        for n in range(27):
            cmain[n * 8 + c] = got[n * 16 : (n + 1) * 16]
            crest[n * 8 + c] = rest[n * 16 : (n + 1) * 16]

    acc[...] = jnp.zeros_like(acc)
    cacc[...] = jnp.zeros_like(cacc)
    group_of_lane = lax.broadcasted_iota(jnp.int32, (16, 128), 1) // 32

    def body(i, tab, octs, slots, n):
        width = -(-slots * 160 // 256) * 256
        rests = -(-slots // 4)
        at = [(i * slots + j) * (2 + n) for j in range(slots)]
        km = [tab[a] for a in at]
        kk = [tab[a + 1] for a in at]
        for j in range(slots):
            lhs[:, j * 128 : (j + 1) * 128] = mbuf[km[j], :, 0:128]
        for g in range(rests):
            parts = [mbuf[km[j], :, 128:Q].astype(F32) for j in range(4 * g, min(4 * g + 4, slots))]
            gap = jnp.zeros((Q, 8), F32)
            parts = [x for part in parts for x in (part, gap)]
            room = 128 - 32 * (len(parts) // 2)
            if room:
                parts.append(jnp.zeros((Q, room), F32))
            lhs[:, (slots + g) * 128 : (slots + g + 1) * 128] = jnp.concatenate(parts, axis=1).astype(BF16)
        if (slots + rests) * 128 < width:
            lhs[:, (slots + rests) * 128 : width] = jnp.zeros((Q, width - (slots + rests) * 128), BF16)
        for pair in range(n // 2):
            buffer = rhs[pair % 2]
            for half in range(2):
                o = octs[i * n + 2 * pair + half]
                cols = slice(half * 128, half * 128 + 128)
                for j in range(slots):
                    w = tab[at[j] + 2 + 2 * pair + half]
                    m = jnp.broadcast_to(mask[o, pl.ds(kk[j], 1), :], (16, 128)).astype(BF16)
                    m8 = jnp.concatenate([m] * 8, axis=0)
                    buffer[j * 128 : (j + 1) * 128, cols] = window[w, 0:128, :] * m8
                    rest_at = slots * 128 + j * 32
                    buffer[rest_at : rest_at + 32, cols] = window[w, 128:160, :] * m8[:32]
            if slots * 160 < width:
                buffer[slots * 160 : width, :] = jnp.zeros((width - slots * 160, 256), BF16)
            got = lax.dot_general(lhs[:, 0:width], buffer[0:width, :], NN, preferred_element_type=F32)
            for half in range(2):
                o = octs[i * n + 2 * pair + half]
                acc[o] += got[:, half * 128 : half * 128 + 128]
        rows = jnp.concatenate([cmask[pl.ds(kk[j], 1), :] for j in range(slots)], axis=0)
        chosen = jnp.concatenate([cpicks[octs[i * n + q]] for q in range(n)], axis=0)
        cm = lax.dot_general(chosen, rows.astype(BF16), NT, preferred_element_type=F32)
        for q in range(n):
            r = slice(q * 16, q * 16 + 16)
            for g in range(rests):
                total = None
                for j in range(4 * g, min(4 * g + 4, slots)):
                    w = tab[at[j] + 2 + q]
                    m = jnp.broadcast_to(cm[r, j : j + 1], (16, 128))
                    crhs[r, j * 128 : (j + 1) * 128] = cmain[w] * m.astype(BF16)
                    m = jnp.where(group_of_lane == j - 4 * g, m, 0.0).astype(BF16)
                    term = crest[w] * m
                    total = term if total is None else total + term
                crhs[r, (slots + g) * 128 : (slots + g + 1) * 128] = total
        if (slots + rests) * 128 < width:
            crhs[:, (slots + rests) * 128 : width] = jnp.zeros((128, width - (slots + rests) * 128), BF16)
        got = lax.dot_general(crhs[0 : n * 16, 0:width], lhs[:, 0:width], NT, preferred_element_type=F32)
        for q in range(n):
            cacc[octs[i * n + q]] += got[q * 16 : q * 16 + 16]

    def eight(i, _):
        for step, planes in enumerate(((1,), (2, 3), (4,), (5, 0, 6))):

            @pl.when(i == step)
            def _(planes=planes):
                for n in planes:
                    loads[n].wait()

        body(i, t8, o8, 25, 8)
        return 0

    lax.fori_loop(0, 4, eight, 0)

    def four(i, _):
        body(i, t4, o4, 25, 4)
        return 0

    lax.fori_loop(0, 6, four, 0)

    def two(i, _):
        body(i, t2, o2, 8, 2)
        return 0

    lax.fori_loop(0, 12, two, 0)

    local_rows = (0.5 * cacc[...].reshape(128, Q)).astype(BF16)
    picks = cpicks[...].reshape(128, 128)
    local = lax.dot_general(local_rows, picks, TN, preferred_element_type=F32).astype(BF16)
    for o in range(8):
        total = acc[o] + lax.dot_general(down[o], local, NN, preferred_element_type=F32)
        density = lax.dot_general(inverse[...], total.astype(BF16), NN, preferred_element_type=F32)
        lhs[:, o * 128 : (o + 1) * 128] = density.astype(BF16)
    out[...] = lax.dot_general(lhs[:, 0:1024], perm[...], NT, preferred_element_type=F32).astype(BF16)


def translate(ef, ec, maps, fine_lists, coarse_lists, down, inverse):
    vmem = pl.BlockSpec(memory_space=pltpu.VMEM)
    smem = pl.BlockSpec(memory_space=pltpu.SMEM)
    tables = [jnp.asarray(part) for members in (EIGHT, FOUR, TWO) for part in table(members)]
    return pl.pallas_call(
        translate_kernel,
        out_shape=jax.ShapeDtypeStruct((Q, 1024), BF16),
        in_specs=[smem] * 6 + [vmem] * 2 + [pl.BlockSpec(memory_space=pl.ANY)] + [vmem] * 8,
        out_specs=vmem,
        scratch_shapes=[
            pltpu.VMEM((OFFS, Q, Q), BF16),
            pltpu.VMEM((216, 160, 128), BF16),
            pltpu.VMEM((216, 16, 128), BF16),
            pltpu.VMEM((216, 16, 128), BF16),
            pltpu.VMEM((8, OFFS + 4, 128), F32),
            pltpu.VMEM((OFFS + 4, 128), F32),
            pltpu.VMEM((1024, 1024), BF16),
            pltpu.VMEM((Q, 4096), BF16),
            [pltpu.VMEM((4096, 256), BF16)] * 2,
            pltpu.VMEM((128, 4096), BF16),
            pltpu.VMEM((8, Q, 128), F32),
            pltpu.VMEM((8, 16, Q), F32),
            pltpu.SemaphoreType.DMA((7,)),
        ],
        compiler_params=pltpu.CompilerParams(vmem_limit_bytes=62 << 20),
        name="translate",
    )(
        *tables, ef, ec, maps, fine_lists, coarse_lists, down, inverse,
        jnp.asarray(window_rows().reshape(1, -1)), jnp.asarray(coarse_window_picks(), BF16),
        jnp.asarray(fine_places()), jnp.asarray(coarse_picks().reshape(8, 16, 128), BF16),
    )


def local(multipole, upward_maps, transfer_maps, downward_maps, check_inverse, fine_lists, coarse_lists):
    ef, ec = exchange(multipole, upward_maps)
    return translate(ef, ec, transfer_maps, fine_lists, coarse_lists, downward_maps, check_inverse)


def solution(mesh):
    placed = (P(None, "curve"), P(), P(), P(), P(), P(None, "curve"), P(None, "curve"))
    return jax.shard_map(local, mesh=mesh, in_specs=placed, out_specs=P(None, "curve"), check_vma=False)
```

time: 736 us -> 151 us (0.21); the launches traced: 722 us -> 150 us
  local copies, waits for them, and re-layouts: 448 us -> 43 us
  matrix products: 164 us -> 0 us
  Pallas kernels: 0 us -> 107 us
  starting transfers between devices: 68.6 us -> 0 us
  waiting for transfers between devices: 25.8 us -> 0 us
  other arithmetic: 12.5 us -> 0 us
    unnamed x1225 -> x13, local copies, waits for them, and re-layouts: 277 us -> 43 us
    dot_general x10 -> x0, matrix products: 164 us -> none  [the longest x7 152 us: translate(): jnp.einsum('kpq,kqb->pb', operators[start_at:start_at + len(chosen)], sta...]
    slice x45 -> x0, local copies, waits for them, and re-layouts: 162 us -> none  [the longest x5 81.6 us: translate(): operators[start_at:start_at + len(chosen)]]
    pallas_call x0 -> x2, Pallas kernels: none -> 107 us  [the longest x1 63.3 us: translate(): pl.pallas_call(translate_kernel, out_shape=jax.ShapeDtypeStruct((Q, 1024)...]
    ppermute x28 -> x0, starting transfers between devices: 68.6 us -> none  [passed_along(): lax.ppermute(shard, axis, [(i, (i + by) % devices) for i in range(devices)])]
    ppermute x28 -> x0, waiting for transfers between devices: 25.8 us -> none  [passed_along(): lax.ppermute(shard, axis, [(i, (i + by) % devices) for i in range(devices)])]
    concatenate x9 -> x0, other arithmetic: 7.75 us -> none  [extend_axis(): jnp.concatenate([received[0], density, received[1]], axis=1 + axis_number)]
  transfers between devices with their start and end apart: 28 -> 0, of which waited for: 8 -> 0; matrix products, arithmetic and copies ran while one was open for 18% -> 0% of each run, Pallas kernels for 0% -> 0%
where the time goes in v1:
time: 151 us; the launch traced here: 150 us
  Pallas kernels  107 us (71%)
  local copies, waits for them, and re-layouts  43 us (28%)
    pallas_call x1, Pallas kernels, translate(): pl.pallas_call(translate_kernel, out_shape=jax.ShapeDtypeStruct((Q, 1024)...  63.3 us
    pallas_call x1, Pallas kernels, exchange(): pl.pallas_call(exchange_kernel, out_shape=[jax.ShapeDtypeStruct((ROWS, 12...  43.3 us
    unnamed x13, local copies, waits for them, and re-layouts  43 us

profile of v1, /device:TPU:1, one launch (start us, length us, event | category | flops | bytes accessed | tf_op | source)
XLA Modules:
  0.0 149.8 jit_solution(7680047936180614463)
XLA Ops:
  0.0 0.0 copy-start.2
  0.0 1.1 copy-done.2
  1.1 0.0 copy-start.3
  1.1 1.0 copy-done.3
  2.0 0.0 copy-start.4
  2.0 0.9 copy-done.4
  3.0 0.0 copy-start.5
  3.0 0.8 copy-done.5
  3.7 43.3 %exchange.1 = (bf16[608,1280]{1,0:T(8,128)(2,1)S(1)}, bf16[27,16,1280]{2,1,0:T(8,128)(2,1)S(1)}) custom-call(bf16[152,1024]{1,0:T(8,128)(2,1)S(1)} %copy-done.3, bf16[8,152,152]{2,1,0:T(8,128)(2,1)S(1)} %copy-done.2, bf16[608,128]{1,0:T(8,128)(2,1)S(1)} %copy-done.4, bf16[128,128]{1,0:T(8,128)(2,1)S(1)} %copy-done.5), custom_call_target="tpu_custom_call" | custom-call | tf_op jit(solution)/shard_map/exchange/pallas_call | solution.py:249
  47.0 0.0 copy-start
  47.0 1.2 copy-done
  48.2 0.0 copy-start.1
  48.2 1.0 copy-done.1
  49.2 37.1 %copy.20.maps = bf16[316,152,152]{2,1,0:T(8,128)(2,1)} copy(bf16[316,152,152]{0,2,1:T(8,128)(2,1)} %param.21) | data formatting | bytes 29203456 | tf_op args[2]
  86.3 63.3 %translate.1 = bf16[152,1024]{1,0:T(8,128)(2,1)} custom-call(s32[1000]{0:T(1024)} %constant.26.clone.t8, s32[32]{0:T(128)} %constant.27.clone.o8, s32[900]{0:T(1024)} %constant.28.clone.t4, s32[24]{0:T(128)} %constant.29.clone.o4, s32[384]{0:T(512)} %constant.30.clone.t2, s32[24]{0:T(128)} %constant.31.clone.o2, bf16[608,1280]{1,0:T(8,128)(2,1)} %copy-done, ...), custom_call_target="tpu_custom_call" | custom-call | tf_op jit(solution)/shard_map/translate/pallas_call | solution.py:435
Async XLA Ops:
  0.0 1.1 copy-start.2
  1.1 1.0 copy-start.3
  2.0 0.9 copy-start.4
  3.0 0.8 copy-start.5
  47.0 1.2 copy-start
  48.2 1.0 copy-start.1

commit v2 on v1

--- a/solution.py
+++ b/solution.py
@@ -12,6 +12,7 @@
 OFFS = 316
 F32 = jnp.float32
 BF16 = jnp.bfloat16
+PAIR, DEEP = 2, 1024
 NN = (((1,), (0,)), ((), ()))
 NT = (((1,), (1,)), ((), ()))
 TN = (((0,), (0,)), ((), ()))
@@ -29,11 +30,20 @@
 OCTANTS = [(a, b, c) for a in (0, 1) for b in (0, 1) for c in (0, 1)]
 
 
-def piece_rows(side):
+FINE = (4, 4, 8)
+COARSE = (2, 2, 4)
+
+
+def piece_rows(side, extents=FINE):
     ranges = []
-    for component, extent in zip(side, (4, 4, 8)):
+    for component, extent in zip(side, extents):
         ranges.append({-1: [extent - 1], 0: list(range(extent)), 1: [0]}[component])
     return [(x, y, z) for x in ranges[0] for y in ranges[1] for z in ranges[2]]
+
+
+def folding(count):
+    tiles = {8: 5, 4: 3, 2: 2, 1: 1}.get(count, 10)
+    return tiles, -(-10 // tiles)
 
 
 def piece_places():
@@ -52,12 +62,24 @@
 SPAN = {-1: (0, OWN + 288), 0: (OWN, OWN + 288), 1: (OWN, ROWS)}
 
 
+def piece_picks(side, extents, size):
+    picks = np.zeros((size, extents[0] * extents[1] * extents[2]), np.float32)
+    rows = piece_rows(side, extents)
+    for fold in range(folding(len(rows))[1]):
+        for number, (x, y, z) in enumerate(rows):
+            picks[fold * len(rows) + number, (x * extents[1] + y) * extents[2] + z] = 1
+    return picks
+
+
 def send_picks():
     picks = np.zeros((ROWS, 128), np.float32)
-    for side, (row, _) in PLACES.items():
-        for number, (x, y, z) in enumerate(piece_rows(side)):
-            picks[row + number, x * 32 + y * 8 + z] = 1
+    for side, (row, size) in PLACES.items():
+        picks[row : row + size] = piece_picks(side, FINE, size)
     return picks
+
+
+def coarse_send_picks():
+    return np.concatenate([piece_picks(side, COARSE, 16) for side in SIDES])
 
 
 def window_rows():
@@ -82,7 +104,7 @@
                     at = (x + shift[0], y + shift[1], z + shift[2])
                     side = tuple((-1 if c < 0 else 1 if c >= e else 0) for c, e in zip(at, (2, 2, 4)))
                     wrapped = tuple(c % e for c, e in zip(at, (2, 2, 4)))
-                    row = SIDES.index(side) * 16 + wrapped[0] * 8 + wrapped[1] * 4 + wrapped[2]
+                    row = SIDES.index(side) * 16 + piece_rows(side, COARSE).index(wrapped)
                     picks[number * 16 + x * 8 + y * 4 + z, row] = 1
     return picks
 
@@ -159,29 +181,72 @@
 
 
 EIGHT, FOUR, TWO = groups()
+
+
 PLANES = [(min(n for n, o in enumerate(SHIFTS) if o[0] == d), sum(o[0] == d for o in SHIFTS)) for d in range(-3, 4)]
 PLANE_ORDER = [1, 2, 3, 4, 5, 0, 6]
 
 
-def neighbour(me, shift):
+def brick_of(me):
     def bit(place):
         return me // 2**place % 2
 
-    x = (bit(2) + 2 * bit(5) + shift[0] + 4) % 4
-    y = (bit(1) + 2 * bit(4) + shift[1] + 4) % 4
-    z = (bit(0) + 2 * bit(3) + 4 * bit(6) + shift[2] + 8) % 8
+    return bit(2) + 2 * bit(5), bit(1) + 2 * bit(4), bit(0) + 2 * bit(3) + 4 * bit(6)
+
+
+def neighbour(me, shift):
+    x, y, z = [(c + d + e) % e for c, d, e in zip(brick_of(me), shift, (4, 4, 8))]
     return (
         z % 2 + 2 * (y % 2) + 4 * (x % 2) + 8 * (z // 2 % 2) + 16 * (y // 2) + 32 * (x // 2) + 64 * (z // 4)
     )
 
 
+def inside(me, shift):
+    found = True
+    for c, d, e in zip(brick_of(me), shift, (4, 4, 8)):
+        if d == 1:
+            found = jnp.logical_and(found, c < e - 1)
+        if d == -1:
+            found = jnp.logical_and(found, c > 0)
+    return found
+
+
+def fold(piece, count):
+    tiles, folds = folding(count)
+    row = lax.broadcasted_iota(jnp.int32, (16, tiles * 128), 0) // count
+    total = jnp.zeros((16, tiles * 128), F32)
+    for number in range(folds):
+        part = piece[:, number * tiles * 128 : min((number + 1) * tiles, 10) * 128]
+        if part.shape[1] < tiles * 128:
+            part = jnp.concatenate([part, jnp.zeros((16, tiles * 128 - part.shape[1]), F32)], axis=1)
+        total = jnp.where(row == number, part, total)
+    return total.astype(BF16)
+
+
+def unfold(piece, count):
+    folds = folding(count)[1]
+    piece = piece.astype(F32)
+    flat = jnp.concatenate([piece[k * count : (k + 1) * count] for k in range(folds)], axis=1)[:, :1280]
+    return jnp.concatenate([flat, jnp.zeros((16 - count, 1280), F32)], axis=0).astype(BF16)
+
+
 def spread_lanes(blocks, copies=False):
     gap = jnp.zeros((blocks[0].shape[0], 8), blocks[0].dtype)
     return jnp.concatenate([part for block in blocks for part in (block, gap)], axis=1)
 
 
-def exchange_kernel(mult, up, picks, cpicks, ef, ec, sent, csent, send, recv, csend, crecv):
+def exchange_kernel(
+    mult, up, picks, cpicks, cends, maps, ef, ec, heads, tails,
+    sent, csent, slab, turned, turned_tail, head, tail, send, recv, csend, crecv, slab_sem, out_sem,
+):
     me = lax.axis_index("curve")
+
+    def fetch(i, size=16):
+        return pltpu.make_async_copy(
+            maps.at[pl.ds(i * 16, size)], slab.at[i % 2, pl.ds(0, size)], slab_sem.at[i % 2]
+        )
+
+    fetch(0).start()
     others = [s for s in SIDES if s != (0, 0, 0)]
     barrier = pltpu.get_barrier_semaphore()
     for side in others:
@@ -198,88 +263,194 @@
         rests.append(child[:, 128:])
         coarse += lax.dot_general(child.astype(BF16), up[o], NT, preferred_element_type=F32)
     ef[OWN : OWN + 128, 1024:1280] = spread_lanes(rests).astype(BF16)
-    sent[...] = lax.dot_general(
-        picks[...], ef[OWN : OWN + 128, :], NN, preferred_element_type=F32
-    ).astype(BF16)
+    folded = [side for side in others if PLACES[side][1] == 16 and len(piece_rows(side)) < 16]
+    for side in others:
+        start, size = PLACES[side]
+        count = len(piece_rows(side))
+        piece = lax.dot_general(
+            picks[start : start + size, :], ef[OWN : OWN + 128, :], NN, preferred_element_type=F32
+        )
+        tiles = folding(count)[0]
+        sent[start : start + size, 0 : tiles * 128] = fold(piece, count) if side in folded else piece.astype(BF16)
+
+        @pl.when(jnp.logical_not(inside(me, side)))
+        def _(start=start, size=size, side=side):
+            ef[start : start + size, :] = jnp.zeros((size, 1280), BF16)
+            ec[SIDES.index(side)] = jnp.zeros((16, 1280), BF16)
 
     pl.semaphore_wait(barrier, 26)
-    copies = []
-    for number, side in enumerate(others):
+
+    def fine_copy(number):
+        side = others[number]
         start, size = PLACES[side]
-        to = neighbour(me, tuple(-c for c in side))
-        copies.append(
-            pltpu.make_async_remote_copy(
-                src_ref=sent.at[pl.ds(start, size)],
-                dst_ref=ef.at[pl.ds(start, size)],
-                send_sem=send.at[number],
-                recv_sem=recv.at[number],
-                device_id=(to,),
-                device_id_type=MESH,
-            )
+        lanes = pl.ds(0, folding(len(piece_rows(side)))[0] * 128)
+        return pltpu.make_async_remote_copy(
+            src_ref=sent.at[pl.ds(start, size), lanes],
+            dst_ref=ef.at[pl.ds(start, size), lanes],
+            send_sem=send.at[number],
+            recv_sem=recv.at[number],
+            device_id=(neighbour(me, tuple(-c for c in side)),),
+            device_id_type=MESH,
         )
-        copies[-1].start()
-
+
+    def coarse_copy(number):
+        side = others[number]
+        lanes = pl.ds(0, folding(len(piece_rows(side, COARSE)))[0] * 128)
+        return pltpu.make_async_remote_copy(
+            src_ref=csent.at[SIDES.index(side), :, lanes],
+            dst_ref=ec.at[SIDES.index(side), :, lanes],
+            send_sem=csend.at[number],
+            recv_sem=crecv.at[number],
+            device_id=(neighbour(me, tuple(-c for c in side)),),
+            device_id_type=MESH,
+        )
+
+    def start_all(copy):
+        for number, side in enumerate(others):
+
+            @pl.when(inside(me, tuple(-c for c in side)))
+            def _(number=number):
+                copy(number).start()
+
+    start_all(fine_copy)
     coarse = coarse.astype(BF16)
     rests = []
     mine = lax.dot_general(cpicks[...], coarse, NN, preferred_element_type=F32)
     for o in range(8):
-        csent[:, o * 128 : (o + 1) * 128] = mine[o * 16 : (o + 1) * 16, :128].astype(BF16)
+        ec[13, :, o * 128 : (o + 1) * 128] = mine[o * 16 : (o + 1) * 16, :128].astype(BF16)
         rests.append(mine[o * 16 : (o + 1) * 16, 128:])
-    csent[:, 1024:1280] = spread_lanes(rests).astype(BF16)
-    for number, side in enumerate(others):
-        to = neighbour(me, tuple(-c for c in side))
-        copies.append(
-            pltpu.make_async_remote_copy(
-                src_ref=csent,
-                dst_ref=ec.at[SIDES.index(side)],
-                send_sem=csend.at[number],
-                recv_sem=crecv.at[number],
-                device_id=(to,),
-                device_id_type=MESH,
-            )
+    ec[13, :, 1024:1280] = spread_lanes(rests).astype(BF16)
+    for side in others:
+        place, count = SIDES.index(side), len(piece_rows(side, COARSE))
+        piece = lax.dot_general(
+            cends[place * 16 : place * 16 + 16, :], ec[13], NN, preferred_element_type=F32
         )
-        copies[-1].start()
-    ec[13] = csent[...]
-    for copy in copies:
-        copy.wait()
-
-
-def exchange(multipole, upward_maps):
+        csent[place, :, 0 : folding(count)[0] * 128] = fold(piece, count)
+    start_all(coarse_copy)
+
+    def leave(i):
+        rows = pl.ds(pl.multiple_of(i * 16, 16), 16)
+        return [
+            pltpu.make_async_copy(head.at[i % 2], heads.at[:, rows], out_sem.at[0, i % 2]),
+            pltpu.make_async_copy(tail.at[i % 2], tails.at[:, rows], out_sem.at[1, i % 2]),
+        ]
+
+    def turn(i):
+        def one(p, _):
+            flat = jnp.swapaxes(slab[i % 2, p].astype(F32), 0, 1)
+            turned[p, 0:OFFS, :] = flat[:, :128]
+            turned_tail[p, 0:OFFS, 0 : Q - 128] = flat[:, 128:]
+            return 0
+
+        lax.fori_loop(0, 16, one, 0, unroll=4)
+
+        def eight(k, _):
+            at = pl.ds(pl.multiple_of(k * 8, 8), 8)
+            head[i % 2, at] = jnp.swapaxes(turned[:, at, :], 0, 1).astype(BF16)
+            tail[i % 2, at] = jnp.swapaxes(turned_tail[:, at, :], 0, 1).astype(BF16)
+            return 0
+
+        lax.fori_loop(0, 40, eight, 0, unroll=5)
+        for part in leave(i):
+            part.start()
+
+    def step(i, _):
+        fetch(i).wait()
+
+        @pl.when(i < 8)
+        def _():
+            fetch(i + 1).start()
+
+        @pl.when(i == 8)
+        def _():
+            fetch(9, 8).start()
+
+        @pl.when(i >= 2)
+        def _():
+            for part in leave(i - 2):
+                part.wait()
+
+        turn(i)
+        return 0
+
+    lax.fori_loop(0, 9, step, 0)
+    fetch(9, 8).wait()
+    for part in leave(7):
+        part.wait()
+    turn(9)
+    for copy in (fine_copy, coarse_copy):
+        for number, side in enumerate(others):
+
+            @pl.when(inside(me, tuple(-c for c in side)))
+            def _(copy=copy, number=number):
+                copy(number).wait_send()
+
+            @pl.when(inside(me, side))
+            def _(copy=copy, number=number):
+                copy(number).wait_recv()
+
+    for side in folded:
+        rows, count = slice(PLACES[side][0], PLACES[side][0] + 16), len(piece_rows(side))
+        ef[rows, :] = unfold(ef[rows, 0 : folding(count)[0] * 128], count)
+    for side in others:
+        place, count = SIDES.index(side), len(piece_rows(side, COARSE))
+        ec[place] = unfold(ec[place, :, 0 : folding(count)[0] * 128], count)
+    for part in leave(8) + leave(9):
+        part.wait()
+
+
+def exchange(multipole, upward_maps, maps):
     vmem = pl.BlockSpec(memory_space=pltpu.VMEM)
     return pl.pallas_call(
         exchange_kernel,
         out_shape=[
             jax.ShapeDtypeStruct((ROWS, 1280), BF16),
             jax.ShapeDtypeStruct((27, 16, 1280), BF16),
+            jax.ShapeDtypeStruct((OFFS + 4, 160, 128), BF16),
+            jax.ShapeDtypeStruct((OFFS + 4, 160, 128), BF16),
         ],
-        in_specs=[vmem] * 4,
-        out_specs=[vmem] * 2,
+        in_specs=[vmem] * 5 + [pl.BlockSpec(memory_space=pl.ANY)],
+        out_specs=[vmem] * 2 + [pl.BlockSpec(memory_space=pl.ANY)] * 2,
         scratch_shapes=[
             pltpu.VMEM((ROWS, 1280), BF16),
-            pltpu.VMEM((16, 1280), BF16),
+            pltpu.VMEM((27, 16, 640), BF16),
+            pltpu.VMEM((2, 16, Q, OFFS), BF16),
+            pltpu.VMEM((16, OFFS + 4, 128), F32),
+            pltpu.VMEM((16, OFFS + 4, 128), F32),
+            pltpu.VMEM((2, OFFS + 4, 16, 128), BF16),
+            pltpu.VMEM((2, OFFS + 4, 16, 128), BF16),
             pltpu.SemaphoreType.DMA((26,)),
             pltpu.SemaphoreType.DMA((26,)),
             pltpu.SemaphoreType.DMA((26,)),
             pltpu.SemaphoreType.DMA((26,)),
+            pltpu.SemaphoreType.DMA((2,)),
+            pltpu.SemaphoreType.DMA((2, 2)),
         ],
         compiler_params=pltpu.CompilerParams(
             collective_id=0, has_side_effects=True, vmem_limit_bytes=40 << 20
         ),
         name="exchange",
-    )(multipole, upward_maps, jnp.asarray(send_picks(), BF16), jnp.asarray(coarse_picks(), BF16))
+    )(
+        multipole, upward_maps, jnp.asarray(send_picks(), BF16), jnp.asarray(coarse_picks(), BF16),
+        jnp.asarray(coarse_send_picks(), BF16), jnp.transpose(maps, (1, 2, 0)),
+    )
 
 
 def translate_kernel(
-    t8, o8, t4, o4, t2, o2, ef, ec, maps, fine_lists, coarse_lists, down, inverse,
+    t8, o8, t4, o4, t2, o2, ef, ec, heads_in, tails_in, fine_lists, coarse_lists, down, inverse,
     wrows, wcpicks, places, cpicks, out,
-    mbuf, window, cmain, crest, mask, cmask, perm, lhs, rhs, crhs, acc, cacc, sems,
+    heads, tails, pick, window, cmain, crest, mask, cmask, perm, lhs, crhs, acc, cacc, sems,
 ):
     loads = [
-        pltpu.make_async_copy(maps.at[pl.ds(*PLANES[n])], mbuf.at[pl.ds(*PLANES[n])], sems.at[n])
+        [
+            pltpu.make_async_copy(heads_in.at[pl.ds(*PLANES[n])], heads.at[pl.ds(*PLANES[n])], sems.at[0, n]),
+            pltpu.make_async_copy(tails_in.at[pl.ds(*PLANES[n])], tails.at[pl.ds(*PLANES[n])], sems.at[1, n]),
+        ]
         for n in range(7)
     ]
     for n in PLANE_ORDER:
-        loads[n].start()
+        for part in loads[n]:
+            part.start()
 
     for at in range(0, 1024, 128):
         box = lax.broadcasted_iota(jnp.int32, (128, 1024), 0) + at
@@ -296,13 +467,21 @@
 
     for dx in (-1, 0, 1):
         first, last = SPAN[dx]
-        iota = lax.broadcasted_iota(jnp.int32, (last - first, 1152), 0) + first
-        pick = (iota == wrows[:, (dx + 1) * 1152 : (dx + 2) * 1152]).astype(F32).astype(BF16)
-
-        def block(i, _, first=first, last=last, pick=pick, dx=dx):
+        span = last - first
+
+        def mark(i, _, first=first, dx=dx):
+            iota = lax.broadcasted_iota(jnp.int32, (16, 1152), 0) + (first + i * 16)
+            wanted = wrows[:, (dx + 1) * 1152 : (dx + 2) * 1152]
+            at = pl.ds(pl.multiple_of(i * 16, 16), 16)
+            pick[at, :] = (iota == wanted).astype(F32).astype(BF16)
+            return 0
+
+        lax.fori_loop(0, span // 16, mark, 0)
+
+        def block(i, _, first=first, last=last, span=span, dx=dx):
             lanes = pl.ds(pl.multiple_of(i * 128, 128), 128)
             got = lax.dot_general(
-                ef[first:last, lanes], pick, TN, preferred_element_type=F32
+                ef[first:last, lanes], pick[0:span, :], TN, preferred_element_type=F32
             ).astype(BF16)
             for n in range(9):
                 window[((dx + 1) * 9 + n) * 8 + i, 0:128, :] = got[:, n * 128 : (n + 1) * 128]
@@ -311,7 +490,7 @@
         lax.fori_loop(0, 8, block, 0)
         for half in range(2):
             got = lax.dot_general(
-                ef[first:last, 1024 + half * 128 : 1152 + half * 128], pick, TN, preferred_element_type=F32
+                ef[first:last, 1024 + half * 128 : 1152 + half * 128], pick[0:span, :], TN, preferred_element_type=F32
             ).astype(BF16)
             for n in range(9):
                 for c in range(4):
@@ -328,50 +507,68 @@
             wcpicks[...], source[:, 1024 + c * 32 : 1056 + c * 32], NN, preferred_element_type=F32
         )
         rest = jnp.concatenate([rest] * 4, axis=1).astype(BF16)
+        group_of_lane = lax.broadcasted_iota(jnp.int32, (16, 128), 1) // 32
         for n in range(27):
             cmain[n * 8 + c] = got[n * 16 : (n + 1) * 16]
-            crest[n * 8 + c] = rest[n * 16 : (n + 1) * 16]
+            for j in range(4):
+                only = (group_of_lane == j).astype(F32).astype(BF16)
+                crest[j, n * 8 + c] = rest[n * 16 : (n + 1) * 16] * only
 
     acc[...] = jnp.zeros_like(acc)
     cacc[...] = jnp.zeros_like(cacc)
-    group_of_lane = lax.broadcasted_iota(jnp.int32, (16, 128), 1) // 32
-
     def body(i, tab, octs, slots, n):
-        width = -(-slots * 160 // 256) * 256
         rests = -(-slots // 4)
+        cut = slots // 2 + 1 if slots > 8 else slots
+        kept = 16 - cut if slots > 8 else rests
+        order = [("head", j) for j in range(cut)] + [("tail", g) for g in range(kept)]
+        order += [("head", j) for j in range(cut, slots)] + [("tail", g) for g in range(kept, rests)]
+        place = {block: number for number, block in enumerate(order)}
+        width = len(order) * 128
         at = [(i * slots + j) * (2 + n) for j in range(slots)]
         km = [tab[a] for a in at]
         kk = [tab[a + 1] for a in at]
+        members = [range(4 * g, min(4 * g + 4, slots)) for g in range(rests)]
+
+        def span(kind, number):
+            return slice(place[kind, number] * 128, place[kind, number] * 128 + 128)
+
         for j in range(slots):
-            lhs[:, j * 128 : (j + 1) * 128] = mbuf[km[j], :, 0:128]
+            lhs[:, span("head", j)] = heads[km[j], 0:Q, :]
         for g in range(rests):
-            parts = [mbuf[km[j], :, 128:Q].astype(F32) for j in range(4 * g, min(4 * g + 4, slots))]
+            parts = [tails[km[j], 0:Q, 0 : Q - 128].astype(F32) for j in members[g]]
             gap = jnp.zeros((Q, 8), F32)
             parts = [x for part in parts for x in (part, gap)]
             room = 128 - 32 * (len(parts) // 2)
             if room:
                 parts.append(jnp.zeros((Q, room), F32))
-            lhs[:, (slots + g) * 128 : (slots + g + 1) * 128] = jnp.concatenate(parts, axis=1).astype(BF16)
-        if (slots + rests) * 128 < width:
-            lhs[:, (slots + rests) * 128 : width] = jnp.zeros((Q, width - (slots + rests) * 128), BF16)
-        for pair in range(n // 2):
-            buffer = rhs[pair % 2]
-            for half in range(2):
-                o = octs[i * n + 2 * pair + half]
-                cols = slice(half * 128, half * 128 + 128)
-                for j in range(slots):
-                    w = tab[at[j] + 2 + 2 * pair + half]
+            lhs[:, span("tail", g)] = jnp.concatenate(parts, axis=1).astype(BF16)
+
+        def shown(q, blocks):
+            o = octs[i * n + q]
+            parts = []
+            for kind, number in blocks:
+                for j in [number] if kind == "head" else members[number]:
+                    w = tab[at[j] + 2 + q]
                     m = jnp.broadcast_to(mask[o, pl.ds(kk[j], 1), :], (16, 128)).astype(BF16)
-                    m8 = jnp.concatenate([m] * 8, axis=0)
-                    buffer[j * 128 : (j + 1) * 128, cols] = window[w, 0:128, :] * m8
-                    rest_at = slots * 128 + j * 32
-                    buffer[rest_at : rest_at + 32, cols] = window[w, 128:160, :] * m8[:32]
-            if slots * 160 < width:
-                buffer[slots * 160 : width, :] = jnp.zeros((width - slots * 160, 256), BF16)
-            got = lax.dot_general(lhs[:, 0:width], buffer[0:width, :], NN, preferred_element_type=F32)
-            for half in range(2):
-                o = octs[i * n + 2 * pair + half]
-                acc[o] += got[:, half * 128 : half * 128 + 128]
+                    if kind == "head":
+                        parts.append(window[w, 0:128, :] * jnp.concatenate([m] * 8, axis=0))
+                    else:
+                        parts.append(window[w, 128:160, :] * jnp.concatenate([m] * 2, axis=0))
+                if kind == "tail" and len(members[number]) < 4:
+                    parts.append(jnp.zeros((128 - 32 * len(members[number]), 128), BF16))
+            return jnp.concatenate(parts, axis=0)
+
+        for q in range(0, n, PAIR):
+            got = None
+            for first in range(0, width, DEEP):
+                last = min(first + DEEP, width)
+                blocks = order[first // 128 : last // 128]
+                masked = jnp.concatenate([shown(q + h, blocks) for h in range(PAIR)], axis=1)
+                term = lax.dot_general(lhs[:, first:last], masked, NN, preferred_element_type=F32)
+                got = term if got is None else got + term
+            for h in range(PAIR):
+                acc[octs[i * n + q + h]] += got[:, h * 128 : h * 128 + 128]
+
         rows = jnp.concatenate([cmask[pl.ds(kk[j], 1), :] for j in range(slots)], axis=0)
         chosen = jnp.concatenate([cpicks[octs[i * n + q]] for q in range(n)], axis=0)
         cm = lax.dot_general(chosen, rows.astype(BF16), NT, preferred_element_type=F32)
@@ -379,16 +576,13 @@
             r = slice(q * 16, q * 16 + 16)
             for g in range(rests):
                 total = None
-                for j in range(4 * g, min(4 * g + 4, slots)):
+                for j in members[g]:
                     w = tab[at[j] + 2 + q]
-                    m = jnp.broadcast_to(cm[r, j : j + 1], (16, 128))
-                    crhs[r, j * 128 : (j + 1) * 128] = cmain[w] * m.astype(BF16)
-                    m = jnp.where(group_of_lane == j - 4 * g, m, 0.0).astype(BF16)
-                    term = crest[w] * m
+                    m = jnp.broadcast_to(cm[r, j : j + 1], (16, 128)).astype(BF16)
+                    crhs[r, span("head", j)] = cmain[w] * m
+                    term = crest[j % 4, w] * m
                     total = term if total is None else total + term
-                crhs[r, (slots + g) * 128 : (slots + g + 1) * 128] = total
-        if (slots + rests) * 128 < width:
-            crhs[:, (slots + rests) * 128 : width] = jnp.zeros((128, width - (slots + rests) * 128), BF16)
+                crhs[r, span("tail", g)] = total
         got = lax.dot_general(crhs[0 : n * 16, 0:width], lhs[:, 0:width], NT, preferred_element_type=F32)
         for q in range(n):
             cacc[octs[i * n + q]] += got[q * 16 : q * 16 + 16]
@@ -399,7 +593,8 @@
             @pl.when(i == step)
             def _(planes=planes):
                 for n in planes:
-                    loads[n].wait()
+                    for part in loads[n]:
+                        part.wait()
 
         body(i, t8, o8, 25, 8)
         return 0
@@ -428,42 +623,43 @@
     out[...] = lax.dot_general(lhs[:, 0:1024], perm[...], NT, preferred_element_type=F32).astype(BF16)
 
 
-def translate(ef, ec, maps, fine_lists, coarse_lists, down, inverse):
+def translate(ef, ec, heads, tails, fine_lists, coarse_lists, down, inverse):
     vmem = pl.BlockSpec(memory_space=pltpu.VMEM)
     smem = pl.BlockSpec(memory_space=pltpu.SMEM)
     tables = [jnp.asarray(part) for members in (EIGHT, FOUR, TWO) for part in table(members)]
     return pl.pallas_call(
         translate_kernel,
         out_shape=jax.ShapeDtypeStruct((Q, 1024), BF16),
-        in_specs=[smem] * 6 + [vmem] * 2 + [pl.BlockSpec(memory_space=pl.ANY)] + [vmem] * 8,
+        in_specs=[smem] * 6 + [vmem] * 2 + [pl.BlockSpec(memory_space=pl.ANY)] * 2 + [vmem] * 8,
         out_specs=vmem,
         scratch_shapes=[
-            pltpu.VMEM((OFFS, Q, Q), BF16),
+            pltpu.VMEM((OFFS + 4, 160, 128), BF16),
+            pltpu.VMEM((OFFS + 4, 160, 128), BF16),
+            pltpu.VMEM((448, 1152), BF16),
             pltpu.VMEM((216, 160, 128), BF16),
             pltpu.VMEM((216, 16, 128), BF16),
-            pltpu.VMEM((216, 16, 128), BF16),
+            pltpu.VMEM((4, 216, 16, 128), BF16),
             pltpu.VMEM((8, OFFS + 4, 128), F32),
             pltpu.VMEM((OFFS + 4, 128), F32),
             pltpu.VMEM((1024, 1024), BF16),
             pltpu.VMEM((Q, 4096), BF16),
-            [pltpu.VMEM((4096, 256), BF16)] * 2,
             pltpu.VMEM((128, 4096), BF16),
             pltpu.VMEM((8, Q, 128), F32),
             pltpu.VMEM((8, 16, Q), F32),
-            pltpu.SemaphoreType.DMA((7,)),
+            pltpu.SemaphoreType.DMA((2, 7)),
         ],
         compiler_params=pltpu.CompilerParams(vmem_limit_bytes=62 << 20),
         name="translate",
     )(
-        *tables, ef, ec, maps, fine_lists, coarse_lists, down, inverse,
+        *tables, ef, ec, heads, tails, fine_lists, coarse_lists, down, inverse,
         jnp.asarray(window_rows().reshape(1, -1)), jnp.asarray(coarse_window_picks(), BF16),
         jnp.asarray(fine_places()), jnp.asarray(coarse_picks().reshape(8, 16, 128), BF16),
     )
 
 
 def local(multipole, upward_maps, transfer_maps, downward_maps, check_inverse, fine_lists, coarse_lists):
-    ef, ec = exchange(multipole, upward_maps)
-    return translate(ef, ec, transfer_maps, fine_lists, coarse_lists, downward_maps, check_inverse)
+    ef, ec, heads, tails = exchange(multipole, upward_maps, transfer_maps)
+    return translate(ef, ec, heads, tails, fine_lists, coarse_lists, downward_maps, check_inverse)
 
 
 def solution(mesh):

time: 151 us -> 96.5 us (0.64)
  local copies, waits for them, and re-layouts: 43 us -> 6.75 us
  Pallas kernels: 107 us -> 89 us
    unnamed x13 -> x14, local copies, waits for them, and re-layouts: 43 us -> 6.75 us
    pallas_call x1, Pallas kernels: 63.3 us -> 53.8 us  [translate(): pl.pallas_call(translate_kernel, out_shape=jax.ShapeDtypeStruct((Q, 1024)...]
    pallas_call x1, Pallas kernels: 43.3 us -> 35.2 us  [exchange(): pl.pallas_call(exchange_kernel, out_shape=[jax.ShapeDtypeStruct((ROWS, 12...]
where the time goes in v2:
time: 96.5 us; the launch traced here: 95.9 us
  Pallas kernels  89 us (92%)
  local copies, waits for them, and re-layouts  6.75 us (7%)
    pallas_call x1, Pallas kernels, translate(): pl.pallas_call(translate_kernel, out_shape=jax.ShapeDtypeStruct((Q, 1024)...  53.8 us
    pallas_call x1, Pallas kernels, exchange(): pl.pallas_call(exchange_kernel, out_shape=[jax.ShapeDtypeStruct((ROWS, 12...  35.2 us
    unnamed x14, local copies, waits for them, and re-layouts  6.75 us

profile of v2, /device:TPU:1, one launch (start us, length us, event | category | flops | bytes accessed | tf_op | source)
XLA Modules:
  0.0 95.9 jit_solution(6384199886155751770)
XLA Ops:
  0.0 0.0 copy-start.2
  0.0 1.1 %copy-done.2 = bf16[8,152,152]{2,1,0:T(8,128)(2,1)S(1)} copy-done((bf16[8,152,152]{2,1,0:T(8,128)(2,1)S(1)}, bf16[8,152,152]{2,1,0:T(8,128)(2,1)}, u32[]{:S(2)}) %copy-start.2) | copy-done | bytes 369688
  1.1 0.0 copy-start.3
  1.1 1.0 %copy-done.3 = bf16[152,1024]{1,0:T(8,128)(2,1)S(1)} copy-done((bf16[152,1024]{1,0:T(8,128)(2,1)S(1)}, bf16[152,1024]{1,0:T(8,128)(2,1)}, u32[]{:S(2)}) %copy-start.3) | copy-done | bytes 311320
  2.0 0.0 copy-start.4
  2.0 0.9 copy-done.4
  3.0 0.0 copy-start.5
  3.0 0.9 copy-done.5
  3.9 0.0 copy-start.6
  3.9 0.8 copy-done.6
  4.6 35.2 %exchange.1 = (bf16[608,1280]{1,0:T(8,128)(2,1)S(1)}, bf16[27,16,1280]{2,1,0:T(8,128)(2,1)S(1)}, bf16[320,160,128]{2,1,0:T(8,128)(2,1)}, bf16[320,160,128]{2,1,0:T(8,128)(2,1)}) custom-call(bf16[152,1024]{1,0:T(8,128)(2,1)S(1)} %copy-done.3, bf16[8,152,152]{2,1,0:T(8,128)(2,1)S(1)} %copy-done.2, bf16[608,128]{1,0:T(8,128)(2,1)S(1)} %copy-done.4, ...), custom_call_target="tpu_custom_call" | custom-call | tf_op jit(solution)/shard_map/exchange/pallas_call | solution.py:404
  39.8 0.0 copy-start
  39.8 1.2 %copy-done = bf16[608,1280]{1,0:T(8,128)(2,1)} copy-done((bf16[608,1280]{1,0:T(8,128)(2,1)}, bf16[608,1280]{1,0:T(8,128)(2,1)S(1)}, u32[]{:S(2)}) %copy-start) | copy-done | bytes 1556504
  41.0 0.0 copy-start.1
  41.0 1.0 %copy-done.1 = bf16[27,16,1280]{2,1,0:T(8,128)(2,1)} copy-done((bf16[27,16,1280]{2,1,0:T(8,128)(2,1)}, bf16[27,16,1280]{2,1,0:T(8,128)(2,1)S(1)}, u32[]{:S(2)}) %copy-start.1) | copy-done | bytes 1105944
  42.0 53.8 %translate.1 = bf16[152,1024]{1,0:T(8,128)(2,1)} custom-call(s32[1000]{0:T(1024)} %constant.29.clone.t8, s32[32]{0:T(128)} %constant.30.clone.o8, s32[900]{0:T(1024)} %constant.31.clone.t4, s32[24]{0:T(128)} %constant.32.clone.o4, s32[384]{0:T(512)} %constant.33.clone.t2, s32[24]{0:T(128)} %constant.34.clone.o2, bf16[608,1280]{1,0:T(8,128)(2,1)} %copy-done, ...), custom_call_target="tpu_custom_call" | custom-call | tf_op jit(solution)/shard_map/translate/pallas_call | solution.py:630
Async XLA Ops:
  0.0 1.1 %copy-start.2 = (bf16[8,152,152]{2,1,0:T(8,128)(2,1)S(1)}, bf16[8,152,152]{2,1,0:T(8,128)(2,1)}, u32[]{:S(2)}) copy-start(bf16[8,152,152]{2,1,0:T(8,128)(2,1)} %up.1) | copy-start | bytes 1108996
  1.1 1.0 %copy-start.3 = (bf16[152,1024]{1,0:T(8,128)(2,1)S(1)}, bf16[152,1024]{1,0:T(8,128)(2,1)}, u32[]{:S(2)}) copy-start(bf16[152,1024]{1,0:T(8,128)(2,1)} %mult.1) | copy-start | bytes 933892
  2.0 0.9 copy-start.4
  3.0 0.9 copy-start.5
  3.9 0.8 copy-start.6
  39.8 1.2 %copy-start = (bf16[608,1280]{1,0:T(8,128)(2,1)}, bf16[608,1280]{1,0:T(8,128)(2,1)S(1)}, u32[]{:S(2)}) copy-start(bf16[608,1280]{1,0:T(8,128)(2,1)S(1)} %get-tuple-element.9.ef) | copy-start | bytes 4669444
  41.0 1.0 %copy-start.1 = (bf16[27,16,1280]{2,1,0:T(8,128)(2,1)}, bf16[27,16,1280]{2,1,0:T(8,128)(2,1)S(1)}, u32[]{:S(2)}) copy-start(bf16[27,16,1280]{2,1,0:T(8,128)(2,1)S(1)} %get-tuple-element.10.ec) | copy-start | bytes 3317764

commit v3 on v2

--- a/solution.py
+++ b/solution.py
@@ -183,6 +183,27 @@
 EIGHT, FOUR, TWO = groups()
 
 
+def coarse_table():
+    return np.array(
+        [
+            window_of(offset or offsets[0], o)
+            for members in (EIGHT, FOUR, TWO)
+            for offsets, _ in members
+            for offset in offsets
+            for o in OCTANTS
+        ],
+        np.int32,
+    )
+
+
+TAILS = [
+    offsets[at : at + 4]
+    for members in (EIGHT, FOUR, TWO)
+    for offsets, _ in members
+    for at in range(0, len(offsets), 4)
+]
+
+
 PLANES = [(min(n for n, o in enumerate(SHIFTS) if o[0] == d), sum(o[0] == d for o in SHIFTS)) for d in range(-3, 4)]
 PLANE_ORDER = [1, 2, 3, 4, 5, 0, 6]
 
@@ -237,7 +258,7 @@
 
 def exchange_kernel(
     mult, up, picks, cpicks, cends, maps, ef, ec, heads, tails,
-    sent, csent, slab, turned, turned_tail, head, tail, send, recv, csend, crecv, slab_sem, out_sem,
+    sent, csent, slab, turned, turned_tail, whole_tail, head, tail, send, recv, csend, crecv, slab_sem, out_sem,
 ):
     me = lax.axis_index("curve")
 
@@ -264,12 +285,11 @@
         coarse += lax.dot_general(child.astype(BF16), up[o], NT, preferred_element_type=F32)
     ef[OWN : OWN + 128, 1024:1280] = spread_lanes(rests).astype(BF16)
     folded = [side for side in others if PLACES[side][1] == 16 and len(piece_rows(side)) < 16]
+    pieces = lax.dot_general(picks[...], ef[OWN : OWN + 128, :], NN, preferred_element_type=F32)
     for side in others:
         start, size = PLACES[side]
         count = len(piece_rows(side))
-        piece = lax.dot_general(
-            picks[start : start + size, :], ef[OWN : OWN + 128, :], NN, preferred_element_type=F32
-        )
+        piece = pieces[start : start + size]
         tiles = folding(count)[0]
         sent[start : start + size, 0 : tiles * 128] = fold(piece, count) if side in folded else piece.astype(BF16)
 
@@ -320,11 +340,10 @@
         ec[13, :, o * 128 : (o + 1) * 128] = mine[o * 16 : (o + 1) * 16, :128].astype(BF16)
         rests.append(mine[o * 16 : (o + 1) * 16, 128:])
     ec[13, :, 1024:1280] = spread_lanes(rests).astype(BF16)
+    pieces = lax.dot_general(cends[...], ec[13], NN, preferred_element_type=F32)
     for side in others:
         place, count = SIDES.index(side), len(piece_rows(side, COARSE))
-        piece = lax.dot_general(
-            cends[place * 16 : place * 16 + 16, :], ec[13], NN, preferred_element_type=F32
-        )
+        piece = pieces[place * 16 : place * 16 + 16]
         csent[place, :, 0 : folding(count)[0] * 128] = fold(piece, count)
     start_all(coarse_copy)
 
@@ -335,27 +354,17 @@
             pltpu.make_async_copy(tail.at[i % 2], tails.at[:, rows], out_sem.at[1, i % 2]),
         ]
 
-    def turn(i):
-        def one(p, _):
-            flat = jnp.swapaxes(slab[i % 2, p].astype(F32), 0, 1)
-            turned[p, 0:OFFS, :] = flat[:, :128]
-            turned_tail[p, 0:OFFS, 0 : Q - 128] = flat[:, 128:]
-            return 0
-
-        lax.fori_loop(0, 16, one, 0, unroll=4)
-
-        def eight(k, _):
-            at = pl.ds(pl.multiple_of(k * 8, 8), 8)
-            head[i % 2, at] = jnp.swapaxes(turned[:, at, :], 0, 1).astype(BF16)
-            tail[i % 2, at] = jnp.swapaxes(turned_tail[:, at, :], 0, 1).astype(BF16)
-            return 0
-
-        lax.fori_loop(0, 40, eight, 0, unroll=5)
-        for part in leave(i):
-            part.start()
+    gap = jnp.zeros((8, OFFS), F32)
+    quarter = lax.broadcasted_iota(jnp.int32, (16, 128), 1) // 32
 
     def step(i, _):
-        fetch(i).wait()
+        @pl.when(i < 9)
+        def _():
+            fetch(i).wait()
+
+        @pl.when(i == 9)
+        def _():
+            fetch(9, 8).wait()
 
         @pl.when(i < 8)
         def _():
@@ -370,14 +379,35 @@
             for part in leave(i - 2):
                 part.wait()
 
-        turn(i)
+        def one(p, _):
+            turned[p, 0:OFFS, :] = jnp.swapaxes(slab[i % 2, p, 0:128], 0, 1).astype(F32)
+            last = slab[i % 2, p, 128:Q].astype(F32)
+            last = jnp.concatenate([last, gap] * 4, axis=0).astype(BF16)
+            turned_tail[p, 0:OFFS, :] = jnp.swapaxes(last, 0, 1).astype(F32)
+            return 0
+
+        lax.fori_loop(0, 16, one, 0, unroll=8)
+
+        def eight(k, _):
+            at = pl.ds(pl.multiple_of(k * 8, 8), 8)
+            head[i % 2, at] = jnp.swapaxes(turned[:, at, :], 0, 1).astype(BF16)
+            whole_tail[at] = jnp.swapaxes(turned_tail[:, at, :], 0, 1)
+            return 0
+
+        lax.fori_loop(0, 40, eight, 0, unroll=10)
+        for number, slots in enumerate(TAILS):
+            total = jnp.zeros((16, 128), F32)
+            for j, offset in enumerate(slots):
+                if offset is not None:
+                    total = jnp.where(quarter == j, whole_tail[NUMBER[offset]], total)
+            tail[i % 2, number] = total.astype(BF16)
+        for part in leave(i):
+            part.start()
         return 0
 
-    lax.fori_loop(0, 9, step, 0)
-    fetch(9, 8).wait()
-    for part in leave(7):
+    lax.fori_loop(0, 10, step, 0)
+    for part in leave(8) + leave(9):
         part.wait()
-    turn(9)
     for copy in (fine_copy, coarse_copy):
         for number, side in enumerate(others):
 
@@ -395,8 +425,6 @@
     for side in others:
         place, count = SIDES.index(side), len(piece_rows(side, COARSE))
         ec[place] = unfold(ec[place, :, 0 : folding(count)[0] * 128], count)
-    for part in leave(8) + leave(9):
-        part.wait()
 
 
 def exchange(multipole, upward_maps, maps):
@@ -407,7 +435,7 @@
             jax.ShapeDtypeStruct((ROWS, 1280), BF16),
             jax.ShapeDtypeStruct((27, 16, 1280), BF16),
             jax.ShapeDtypeStruct((OFFS + 4, 160, 128), BF16),
-            jax.ShapeDtypeStruct((OFFS + 4, 160, 128), BF16),
+            jax.ShapeDtypeStruct((len(TAILS), 160, 128), BF16),
         ],
         in_specs=[vmem] * 5 + [pl.BlockSpec(memory_space=pl.ANY)],
         out_specs=[vmem] * 2 + [pl.BlockSpec(memory_space=pl.ANY)] * 2,
@@ -417,8 +445,9 @@
             pltpu.VMEM((2, 16, Q, OFFS), BF16),
             pltpu.VMEM((16, OFFS + 4, 128), F32),
             pltpu.VMEM((16, OFFS + 4, 128), F32),
+            pltpu.VMEM((OFFS + 4, 16, 128), F32),
             pltpu.VMEM((2, OFFS + 4, 16, 128), BF16),
-            pltpu.VMEM((2, OFFS + 4, 16, 128), BF16),
+            pltpu.VMEM((2, len(TAILS), 16, 128), BF16),
             pltpu.SemaphoreType.DMA((26,)),
             pltpu.SemaphoreType.DMA((26,)),
             pltpu.SemaphoreType.DMA((26,)),
@@ -437,20 +466,18 @@
 
 
 def translate_kernel(
-    t8, o8, t4, o4, t2, o2, ef, ec, heads_in, tails_in, fine_lists, coarse_lists, down, inverse,
+    t8, o8, t4, o4, t2, o2, tc, ef, ec, heads_in, tails_in, fine_lists, coarse_lists, down, inverse,
     wrows, wcpicks, places, cpicks, out,
-    heads, tails, pick, window, cmain, crest, mask, cmask, perm, lhs, crhs, acc, cacc, sems,
+    heads, tails, pick, window, cmain, crest, mask, cmask, perm, lhs, acc, cacc, sems,
 ):
     loads = [
-        [
-            pltpu.make_async_copy(heads_in.at[pl.ds(*PLANES[n])], heads.at[pl.ds(*PLANES[n])], sems.at[0, n]),
-            pltpu.make_async_copy(tails_in.at[pl.ds(*PLANES[n])], tails.at[pl.ds(*PLANES[n])], sems.at[1, n]),
-        ]
+        pltpu.make_async_copy(heads_in.at[pl.ds(*PLANES[n])], heads.at[pl.ds(*PLANES[n])], sems.at[n])
         for n in range(7)
     ]
+    load_tails = pltpu.make_async_copy(tails_in, tails, sems.at[7])
+    load_tails.start()
     for n in PLANE_ORDER:
-        for part in loads[n]:
-            part.start()
+        loads[n].start()
 
     for at in range(0, 1024, 128):
         box = lax.broadcasted_iota(jnp.int32, (128, 1024), 0) + at
@@ -462,7 +489,9 @@
             present, perm[:, o * 128 : (o + 1) * 128], NN, preferred_element_type=F32
         )
         mask[o, OFFS : OFFS + 4, :] = jnp.zeros((4, 128), F32)
-    cmask[0:OFFS, :] = (coarse_lists[...] >= 0).astype(F32)
+    picks = cpicks[...].reshape(128, 128)
+    present = (coarse_lists[...] >= 0).astype(F32).astype(BF16)
+    cmask[0:OFFS, :] = lax.dot_general(present, picks, NT, preferred_element_type=F32)
     cmask[OFFS : OFFS + 4, :] = jnp.zeros((4, 128), F32)
 
     for dx in (-1, 0, 1):
@@ -516,7 +545,7 @@
 
     acc[...] = jnp.zeros_like(acc)
     cacc[...] = jnp.zeros_like(cacc)
-    def body(i, tab, octs, slots, n):
+    def body(i, tab, octs, slots, n, first_tail, first_slot):
         rests = -(-slots // 4)
         cut = slots // 2 + 1 if slots > 8 else slots
         kept = 16 - cut if slots > 8 else rests
@@ -535,13 +564,7 @@
         for j in range(slots):
             lhs[:, span("head", j)] = heads[km[j], 0:Q, :]
         for g in range(rests):
-            parts = [tails[km[j], 0:Q, 0 : Q - 128].astype(F32) for j in members[g]]
-            gap = jnp.zeros((Q, 8), F32)
-            parts = [x for part in parts for x in (part, gap)]
-            room = 128 - 32 * (len(parts) // 2)
-            if room:
-                parts.append(jnp.zeros((Q, room), F32))
-            lhs[:, span("tail", g)] = jnp.concatenate(parts, axis=1).astype(BF16)
+            lhs[:, span("tail", g)] = tails[first_tail + i * rests + g, 0:Q, :]
 
         def shown(q, blocks):
             o = octs[i * n + q]
@@ -569,23 +592,21 @@
             for h in range(PAIR):
                 acc[octs[i * n + q + h]] += got[:, h * 128 : h * 128 + 128]
 
-        rows = jnp.concatenate([cmask[pl.ds(kk[j], 1), :] for j in range(slots)], axis=0)
-        chosen = jnp.concatenate([cpicks[octs[i * n + q]] for q in range(n)], axis=0)
-        cm = lax.dot_general(chosen, rows.astype(BF16), NT, preferred_element_type=F32)
-        for q in range(n):
-            r = slice(q * 16, q * 16 + 16)
-            for g in range(rests):
-                total = None
-                for j in members[g]:
-                    w = tab[at[j] + 2 + q]
-                    m = jnp.broadcast_to(cm[r, j : j + 1], (16, 128)).astype(BF16)
-                    crhs[r, span("head", j)] = cmain[w] * m
-                    term = crest[j % 4, w] * m
-                    total = term if total is None else total + term
-                crhs[r, span("tail", g)] = total
-        got = lax.dot_general(crhs[0 : n * 16, 0:width], lhs[:, 0:width], NT, preferred_element_type=F32)
-        for q in range(n):
-            cacc[octs[i * n + q]] += got[q * 16 : q * 16 + 16]
+        total = jnp.zeros((Q, 128), F32)
+        for j in range(slots):
+            first = (first_slot + i * slots + j) * 8
+            ws = [tc[first + q] for q in range(8)]
+            seen = jnp.concatenate(
+                [
+                    jnp.concatenate([cmain[w] for w in ws], axis=0),
+                    jnp.concatenate([crest[j % 4, w] for w in ws], axis=0),
+                ],
+                axis=1,
+            )
+            both = jnp.concatenate([lhs[:, span("head", j)], lhs[:, span("tail", j // 4)]], axis=1)
+            term = lax.dot_general(both, seen, NT, preferred_element_type=F32)
+            total += term * cmask[pl.ds(kk[j], 1), :]
+        cacc[...] += total
 
     def eight(i, _):
         for step, planes in enumerate(((1,), (2, 3), (4,), (5, 0, 6))):
@@ -593,29 +614,29 @@
             @pl.when(i == step)
             def _(planes=planes):
                 for n in planes:
-                    for part in loads[n]:
-                        part.wait()
-
-        body(i, t8, o8, 25, 8)
+                    loads[n].wait()
+
+        body(i, t8, o8, 25, 8, 0, 0)
         return 0
 
+    load_tails.wait()
     lax.fori_loop(0, 4, eight, 0)
 
     def four(i, _):
-        body(i, t4, o4, 25, 4)
+        body(i, t4, o4, 25, 4, 28, 100)
         return 0
 
     lax.fori_loop(0, 6, four, 0)
 
     def two(i, _):
-        body(i, t2, o2, 8, 2)
+        body(i, t2, o2, 8, 2, 70, 250)
         return 0
 
     lax.fori_loop(0, 12, two, 0)
 
-    local_rows = (0.5 * cacc[...].reshape(128, Q)).astype(BF16)
-    picks = cpicks[...].reshape(128, 128)
-    local = lax.dot_general(local_rows, picks, TN, preferred_element_type=F32).astype(BF16)
+    local = lax.dot_general(
+        (0.5 * cacc[...]).astype(BF16), picks, NN, preferred_element_type=F32
+    ).astype(BF16)
     for o in range(8):
         total = acc[o] + lax.dot_general(down[o], local, NN, preferred_element_type=F32)
         density = lax.dot_general(inverse[...], total.astype(BF16), NN, preferred_element_type=F32)
@@ -630,11 +651,11 @@
     return pl.pallas_call(
         translate_kernel,
         out_shape=jax.ShapeDtypeStruct((Q, 1024), BF16),
-        in_specs=[smem] * 6 + [vmem] * 2 + [pl.BlockSpec(memory_space=pl.ANY)] * 2 + [vmem] * 8,
+        in_specs=[smem] * 7 + [vmem] * 2 + [pl.BlockSpec(memory_space=pl.ANY)] * 2 + [vmem] * 8,
         out_specs=vmem,
         scratch_shapes=[
             pltpu.VMEM((OFFS + 4, 160, 128), BF16),
-            pltpu.VMEM((OFFS + 4, 160, 128), BF16),
+            pltpu.VMEM((len(TAILS), 160, 128), BF16),
             pltpu.VMEM((448, 1152), BF16),
             pltpu.VMEM((216, 160, 128), BF16),
             pltpu.VMEM((216, 16, 128), BF16),
@@ -643,15 +664,14 @@
             pltpu.VMEM((OFFS + 4, 128), F32),
             pltpu.VMEM((1024, 1024), BF16),
             pltpu.VMEM((Q, 4096), BF16),
-            pltpu.VMEM((128, 4096), BF16),
             pltpu.VMEM((8, Q, 128), F32),
-            pltpu.VMEM((8, 16, Q), F32),
-            pltpu.SemaphoreType.DMA((2, 7)),
+            pltpu.VMEM((Q, 128), F32),
+            pltpu.SemaphoreType.DMA((8,)),
         ],
         compiler_params=pltpu.CompilerParams(vmem_limit_bytes=62 << 20),
         name="translate",
     )(
-        *tables, ef, ec, heads, tails, fine_lists, coarse_lists, down, inverse,
+        *tables, jnp.asarray(coarse_table()), ef, ec, heads, tails, fine_lists, coarse_lists, down, inverse,
         jnp.asarray(window_rows().reshape(1, -1)), jnp.asarray(coarse_window_picks(), BF16),
         jnp.asarray(fine_places()), jnp.asarray(coarse_picks().reshape(8, 16, 128), BF16),
     )

time: 96.5 us -> 85.9 us (0.89)
  Pallas kernels: 89 us -> 76.9 us
  local copies, waits for them, and re-layouts: 6.75 us -> 8.58 us
    pallas_call x1, Pallas kernels: 53.8 us -> 44.2 us  [translate(): pl.pallas_call(translate_kernel, out_shape=jax.ShapeDtypeStruct((Q, 1024)...]
    pallas_call x1, Pallas kernels: 35.2 us -> 32.7 us  [exchange(): pl.pallas_call(exchange_kernel, out_shape=[jax.ShapeDtypeStruct((ROWS, 12...]
    unnamed x14 -> x16, local copies, waits for them, and re-layouts: 6.75 us -> 8.58 us
where the time goes in v3:
time: 85.9 us; the launch traced here: 85.6 us
  Pallas kernels  76.9 us (90%)
  local copies, waits for them, and re-layouts  8.58 us (10%)
    pallas_call x1, Pallas kernels, translate(): pl.pallas_call(translate_kernel, out_shape=jax.ShapeDtypeStruct((Q, 1024)...  44.2 us
    pallas_call x1, Pallas kernels, exchange(): pl.pallas_call(exchange_kernel, out_shape=[jax.ShapeDtypeStruct((ROWS, 12...  32.7 us
    unnamed x16, local copies, waits for them, and re-layouts  8.58 us

profile of v3, /device:TPU:1, one launch (start us, length us, event | category | flops | bytes accessed | tf_op | source)
XLA Modules:
  0.0 85.6 jit_solution(10052353166217118891)
XLA Ops:
  0.0 0.0 copy-start.3
  0.0 1.1 %copy-done.3 = bf16[8,152,152]{2,1,0:T(8,128)(2,1)S(1)} copy-done((bf16[8,152,152]{2,1,0:T(8,128)(2,1)S(1)}, bf16[8,152,152]{2,1,0:T(8,128)(2,1)}, u32[]{:S(2)}) %copy-start.3) | copy-done | bytes 369688
  1.1 0.0 copy-start.4
  1.1 1.0 %copy-done.4 = bf16[152,1024]{1,0:T(8,128)(2,1)S(1)} copy-done((bf16[152,1024]{1,0:T(8,128)(2,1)S(1)}, bf16[152,1024]{1,0:T(8,128)(2,1)}, u32[]{:S(2)}) %copy-start.4) | copy-done | bytes 311320
  2.0 0.0 copy-start.5
  2.0 0.9 %copy-done.5 = bf16[608,128]{1,0:T(8,128)(2,1)S(1)} copy-done((bf16[608,128]{1,0:T(8,128)(2,1)S(1)}, bf16[608,128]{1,0:T(8,128)(2,1)}, u32[]{:S(2)}) %copy-start.5) | copy-done | bytes 155672
  3.0 0.0 copy-start.6
  3.0 0.9 %copy-done.6 = bf16[432,16]{1,0:T(8,128)(2,1)S(1)} copy-done((bf16[432,16]{1,0:T(8,128)(2,1)S(1)}, bf16[432,16]{1,0:T(8,128)(2,1)}, u32[]{:S(2)}) %copy-start.6) | copy-done | bytes 13848
  3.9 0.0 copy-start.7
  3.9 0.8 copy-done.7
  4.6 32.7 %exchange.1 = (bf16[608,1280]{1,0:T(8,128)(2,1)S(1)}, bf16[27,16,1280]{2,1,0:T(8,128)(2,1)S(1)}, bf16[320,160,128]{2,1,0:T(8,128)(2,1)}, bf16[94,160,128]{2,1,0:T(8,128)(2,1)S(1)}) custom-call(bf16[152,1024]{1,0:T(8,128)(2,1)S(1)} %copy-done.4, bf16[8,152,152]{2,1,0:T(8,128)(2,1)S(1)} %copy-done.3, bf16[608,128]{1,0:T(8,128)(2,1)S(1)} %copy-done.5, ...), custom_call_target="tpu_custom_call" | custom-call | tf_op jit(solution)/shard_map/exchange/pallas_call | solution.py:432
  37.3 0.0 copy-start
  37.4 1.8 %copy-done = bf16[94,160,128]{2,1,0:T(8,128)(2,1)} copy-done((bf16[94,160,128]{2,1,0:T(8,128)(2,1)}, bf16[94,160,128]{2,1,0:T(8,128)(2,1)S(1)}, u32[]{:S(2)}) %copy-start) | copy-done | bytes 3850264
  39.2 0.0 copy-start.1
  39.2 1.2 %copy-done.1 = bf16[608,1280]{1,0:T(8,128)(2,1)} copy-done((bf16[608,1280]{1,0:T(8,128)(2,1)}, bf16[608,1280]{1,0:T(8,128)(2,1)S(1)}, u32[]{:S(2)}) %copy-start.1) | copy-done | bytes 1556504
  40.3 0.0 copy-start.2
  40.3 1.0 %copy-done.2 = bf16[27,16,1280]{2,1,0:T(8,128)(2,1)} copy-done((bf16[27,16,1280]{2,1,0:T(8,128)(2,1)}, bf16[27,16,1280]{2,1,0:T(8,128)(2,1)S(1)}, u32[]{:S(2)}) %copy-start.2) | copy-done | bytes 1105944
  41.3 44.2 %translate.1 = bf16[152,1024]{1,0:T(8,128)(2,1)} custom-call(s32[1000]{0:T(1024)} %constant.31.clone.t8, s32[32]{0:T(128)} %constant.32.clone.o8, s32[900]{0:T(1024)} %constant.33.clone.t4, s32[24]{0:T(128)} %constant.34.clone.o4, s32[384]{0:T(512)} %constant.35.clone.t2, s32[24]{0:T(128)} %constant.36.clone.o2, s32[2768]{0:T(1024)} %constant.37.clone.tc, ...), custom_call_target="tpu_custom_call" | custom-call | tf_op jit(solution)/shard_map/translate/pallas_call | solution.py:651
Async XLA Ops:
  0.0 1.1 %copy-start.3 = (bf16[8,152,152]{2,1,0:T(8,128)(2,1)S(1)}, bf16[8,152,152]{2,1,0:T(8,128)(2,1)}, u32[]{:S(2)}) copy-start(bf16[8,152,152]{2,1,0:T(8,128)(2,1)} %up.1) | copy-start | bytes 1108996
  1.1 1.0 %copy-start.4 = (bf16[152,1024]{1,0:T(8,128)(2,1)S(1)}, bf16[152,1024]{1,0:T(8,128)(2,1)}, u32[]{:S(2)}) copy-start(bf16[152,1024]{1,0:T(8,128)(2,1)} %mult.1) | copy-start | bytes 933892
  2.0 0.9 %copy-start.5 = (bf16[608,128]{1,0:T(8,128)(2,1)S(1)}, bf16[608,128]{1,0:T(8,128)(2,1)}, u32[]{:S(2)}) copy-start(bf16[608,128]{1,0:T(8,128)(2,1)} %constant.28.clone.picks) | copy-start | bytes 466948
  3.0 0.9 %copy-start.6 = (bf16[432,16]{1,0:T(8,128)(2,1)S(1)}, bf16[432,16]{1,0:T(8,128)(2,1)}, u32[]{:S(2)}) copy-start(bf16[432,16]{1,0:T(8,128)(2,1)} %constant.30.clone.cends) | copy-start | bytes 41476
  3.9 0.8 copy-start.7
  37.3 1.8 %copy-start = (bf16[94,160,128]{2,1,0:T(8,128)(2,1)}, bf16[94,160,128]{2,1,0:T(8,128)(2,1)S(1)}, u32[]{:S(2)}) copy-start(bf16[94,160,128]{2,1,0:T(8,128)(2,1)S(1)} %get-tuple-element.12.tails_in) | copy-start | bytes 11550724
  39.2 1.2 %copy-start.1 = (bf16[608,1280]{1,0:T(8,128)(2,1)}, bf16[608,1280]{1,0:T(8,128)(2,1)S(1)}, u32[]{:S(2)}) copy-start(bf16[608,1280]{1,0:T(8,128)(2,1)S(1)} %get-tuple-element.9.ef) | copy-start | bytes 4669444
  40.3 1.0 %copy-start.2 = (bf16[27,16,1280]{2,1,0:T(8,128)(2,1)}, bf16[27,16,1280]{2,1,0:T(8,128)(2,1)S(1)}, u32[]{:S(2)}) copy-start(bf16[27,16,1280]{2,1,0:T(8,128)(2,1)S(1)} %get-tuple-element.10.ec) | copy-start | bytes 3317764

commit v4 on v3

--- a/solution.py
+++ b/solution.py
@@ -12,7 +12,7 @@
 OFFS = 316
 F32 = jnp.float32
 BF16 = jnp.bfloat16
-PAIR, DEEP = 2, 1024
+PAIR, DEEP = 2, 512
 NN = (((1,), (0,)), ((), ()))
 NT = (((1,), (1,)), ((), ()))
 TN = (((0,), (0,)), ((), ()))
@@ -386,7 +386,7 @@
             turned_tail[p, 0:OFFS, :] = jnp.swapaxes(last, 0, 1).astype(F32)
             return 0
 
-        lax.fori_loop(0, 16, one, 0, unroll=8)
+        lax.fori_loop(0, 16, one, 0, unroll=16)
 
         def eight(k, _):
             at = pl.ds(pl.multiple_of(k * 8, 8), 8)
@@ -394,7 +394,7 @@
             whole_tail[at] = jnp.swapaxes(turned_tail[:, at, :], 0, 1)
             return 0
 
-        lax.fori_loop(0, 40, eight, 0, unroll=10)
+        lax.fori_loop(0, 40, eight, 0, unroll=20)
         for number, slots in enumerate(TAILS):
             total = jnp.zeros((16, 128), F32)
             for j, offset in enumerate(slots):
@@ -505,7 +505,7 @@
             pick[at, :] = (iota == wanted).astype(F32).astype(BF16)
             return 0
 
-        lax.fori_loop(0, span // 16, mark, 0)
+        lax.fori_loop(0, span // 16, mark, 0, unroll=2)
 
         def block(i, _, first=first, last=last, span=span, dx=dx):
             lanes = pl.ds(pl.multiple_of(i * 128, 128), 128)
@@ -516,7 +516,7 @@
                 window[((dx + 1) * 9 + n) * 8 + i, 0:128, :] = got[:, n * 128 : (n + 1) * 128]
             return 0
 
-        lax.fori_loop(0, 8, block, 0)
+        lax.fori_loop(0, 8, block, 0, unroll=8)
         for half in range(2):
             got = lax.dot_general(
                 ef[first:last, 1024 + half * 128 : 1152 + half * 128], pick[0:span, :], TN, preferred_element_type=F32
@@ -632,7 +632,7 @@
         body(i, t2, o2, 8, 2, 70, 250)
         return 0
 
-    lax.fori_loop(0, 12, two, 0)
+    lax.fori_loop(0, 12, two, 0, unroll=2)
 
     local = lax.dot_general(
         (0.5 * cacc[...]).astype(BF16), picks, NN, preferred_element_type=F32

time: 85.9 us -> 79.3 us (0.923)
  Pallas kernels: 76.9 us -> 70.3 us
    pallas_call x1, Pallas kernels: 44.2 us -> 38.4 us  [translate(): pl.pallas_call(translate_kernel, out_shape=jax.ShapeDtypeStruct((Q, 1024)...]
    pallas_call x1, Pallas kernels: 32.7 us -> 31.8 us  [exchange(): pl.pallas_call(exchange_kernel, out_shape=[jax.ShapeDtypeStruct((ROWS, 12...]
where the time goes in v4:
time: 79.3 us; the launch traced here: 79 us
  Pallas kernels  70.3 us (89%)
  local copies, waits for them, and re-layouts  8.58 us (11%)
    pallas_call x1, Pallas kernels, translate(): pl.pallas_call(translate_kernel, out_shape=jax.ShapeDtypeStruct((Q, 1024)...  38.4 us
    pallas_call x1, Pallas kernels, exchange(): pl.pallas_call(exchange_kernel, out_shape=[jax.ShapeDtypeStruct((ROWS, 12...  31.8 us
    unnamed x16, local copies, waits for them, and re-layouts  8.58 us

profile of v4, /device:TPU:1, one launch (start us, length us, event | category | flops | bytes accessed | tf_op | source)
XLA Modules:
  0.0 79.0 jit_solution(14680914667565222874)
XLA Ops:
  0.0 0.0 copy-start.3
  0.0 1.1 %copy-done.3 = bf16[8,152,152]{2,1,0:T(8,128)(2,1)S(1)} copy-done((bf16[8,152,152]{2,1,0:T(8,128)(2,1)S(1)}, bf16[8,152,152]{2,1,0:T(8,128)(2,1)}, u32[]{:S(2)}) %copy-start.3) | copy-done | bytes 369688
  1.1 0.0 copy-start.4
  1.1 1.0 %copy-done.4 = bf16[152,1024]{1,0:T(8,128)(2,1)S(1)} copy-done((bf16[152,1024]{1,0:T(8,128)(2,1)S(1)}, bf16[152,1024]{1,0:T(8,128)(2,1)}, u32[]{:S(2)}) %copy-start.4) | copy-done | bytes 311320
  2.0 0.0 copy-start.5
  2.0 0.9 %copy-done.5 = bf16[608,128]{1,0:T(8,128)(2,1)S(1)} copy-done((bf16[608,128]{1,0:T(8,128)(2,1)S(1)}, bf16[608,128]{1,0:T(8,128)(2,1)}, u32[]{:S(2)}) %copy-start.5) | copy-done | bytes 155672
  3.0 0.0 copy-start.6
  3.0 0.9 %copy-done.6 = bf16[432,16]{1,0:T(8,128)(2,1)S(1)} copy-done((bf16[432,16]{1,0:T(8,128)(2,1)S(1)}, bf16[432,16]{1,0:T(8,128)(2,1)}, u32[]{:S(2)}) %copy-start.6) | copy-done | bytes 13848
  3.9 0.0 copy-start.7
  3.9 0.8 copy-done.7
  4.6 31.8 %exchange.1 = (bf16[608,1280]{1,0:T(8,128)(2,1)S(1)}, bf16[27,16,1280]{2,1,0:T(8,128)(2,1)S(1)}, bf16[320,160,128]{2,1,0:T(8,128)(2,1)}, bf16[94,160,128]{2,1,0:T(8,128)(2,1)S(1)}) custom-call(bf16[152,1024]{1,0:T(8,128)(2,1)S(1)} %copy-done.4, bf16[8,152,152]{2,1,0:T(8,128)(2,1)S(1)} %copy-done.3, bf16[608,128]{1,0:T(8,128)(2,1)S(1)} %copy-done.5, ...), custom_call_target="tpu_custom_call" | custom-call | tf_op jit(solution)/shard_map/exchange/pallas_call | solution.py:432
  36.5 0.0 copy-start
  36.5 1.8 %copy-done = bf16[94,160,128]{2,1,0:T(8,128)(2,1)} copy-done((bf16[94,160,128]{2,1,0:T(8,128)(2,1)}, bf16[94,160,128]{2,1,0:T(8,128)(2,1)S(1)}, u32[]{:S(2)}) %copy-start) | copy-done | bytes 3850264
  38.3 0.0 copy-start.1
  38.3 1.2 %copy-done.1 = bf16[608,1280]{1,0:T(8,128)(2,1)} copy-done((bf16[608,1280]{1,0:T(8,128)(2,1)}, bf16[608,1280]{1,0:T(8,128)(2,1)S(1)}, u32[]{:S(2)}) %copy-start.1) | copy-done | bytes 1556504
  39.4 0.0 copy-start.2
  39.4 1.0 %copy-done.2 = bf16[27,16,1280]{2,1,0:T(8,128)(2,1)} copy-done((bf16[27,16,1280]{2,1,0:T(8,128)(2,1)}, bf16[27,16,1280]{2,1,0:T(8,128)(2,1)S(1)}, u32[]{:S(2)}) %copy-start.2) | copy-done | bytes 1105944
  40.4 38.4 %translate.1 = bf16[152,1024]{1,0:T(8,128)(2,1)} custom-call(s32[1000]{0:T(1024)} %constant.31.clone.t8, s32[32]{0:T(128)} %constant.32.clone.o8, s32[900]{0:T(1024)} %constant.33.clone.t4, s32[24]{0:T(128)} %constant.34.clone.o4, s32[384]{0:T(512)} %constant.35.clone.t2, s32[24]{0:T(128)} %constant.36.clone.o2, s32[2768]{0:T(1024)} %constant.37.clone.tc, ...), custom_call_target="tpu_custom_call" | custom-call | tf_op jit(solution)/shard_map/translate/pallas_call | solution.py:651
Async XLA Ops:
  0.0 1.1 %copy-start.3 = (bf16[8,152,152]{2,1,0:T(8,128)(2,1)S(1)}, bf16[8,152,152]{2,1,0:T(8,128)(2,1)}, u32[]{:S(2)}) copy-start(bf16[8,152,152]{2,1,0:T(8,128)(2,1)} %up.1) | copy-start | bytes 1108996
  1.1 1.0 %copy-start.4 = (bf16[152,1024]{1,0:T(8,128)(2,1)S(1)}, bf16[152,1024]{1,0:T(8,128)(2,1)}, u32[]{:S(2)}) copy-start(bf16[152,1024]{1,0:T(8,128)(2,1)} %mult.1) | copy-start | bytes 933892
  2.0 0.9 %copy-start.5 = (bf16[608,128]{1,0:T(8,128)(2,1)S(1)}, bf16[608,128]{1,0:T(8,128)(2,1)}, u32[]{:S(2)}) copy-start(bf16[608,128]{1,0:T(8,128)(2,1)} %constant.28.clone.picks) | copy-start | bytes 466948
  3.0 0.9 %copy-start.6 = (bf16[432,16]{1,0:T(8,128)(2,1)S(1)}, bf16[432,16]{1,0:T(8,128)(2,1)}, u32[]{:S(2)}) copy-start(bf16[432,16]{1,0:T(8,128)(2,1)} %constant.30.clone.cends) | copy-start | bytes 41476
  3.9 0.8 copy-start.7
  36.5 1.8 %copy-start = (bf16[94,160,128]{2,1,0:T(8,128)(2,1)}, bf16[94,160,128]{2,1,0:T(8,128)(2,1)S(1)}, u32[]{:S(2)}) copy-start(bf16[94,160,128]{2,1,0:T(8,128)(2,1)S(1)} %get-tuple-element.12.tails_in) | copy-start | bytes 11550724
  38.3 1.2 %copy-start.1 = (bf16[608,1280]{1,0:T(8,128)(2,1)}, bf16[608,1280]{1,0:T(8,128)(2,1)S(1)}, u32[]{:S(2)}) copy-start(bf16[608,1280]{1,0:T(8,128)(2,1)S(1)} %get-tuple-element.9.ef) | copy-start | bytes 4669444
  39.4 1.0 %copy-start.2 = (bf16[27,16,1280]{2,1,0:T(8,128)(2,1)}, bf16[27,16,1280]{2,1,0:T(8,128)(2,1)S(1)}, u32[]{:S(2)}) copy-start(bf16[27,16,1280]{2,1,0:T(8,128)(2,1)S(1)} %get-tuple-element.10.ec) | copy-start | bytes 3317764
